TPU v7x, 32 devices: a whole 2x2x4 slice. The times are simulated.
32 devices in a mesh: frame: 16 (over z, y, x), head: 2 (over core).
Axes of the slice: x: 2, y: 2, z: 4, core: 2. Of those that a mesh axis runs over, the one named last changes fastest.
Arguments:
- queries: bfloat16 [4096, 5120], P('frame', 'head'), may hold values from -12 to 12
- keys: bfloat16 [4096, 5120], P('frame', 'head'), may hold values from -12 to 12
- values: bfloat16 [4096, 5120], P('frame', 'head'), may hold values from -6 to 6
- policy_grad: bfloat16 [4096, 5120], P('frame', 'head'), may hold values from -6 to 6
- ref_velocity: bfloat16 [4096, 5120], P('frame', 'head'), may hold values from -6 to 6
- key_lists: int32 [32, 6], P('frame'), may hold values from 0 to 31, as said below
- frame_tokens: int32 [32], replicated, may hold values from 32 to 128, as said below
Outputs:
- grad_queries: bfloat16 [4096, 5120], P('frame', 'head')
- grad_keys: bfloat16 [4096, 5120], P('frame', 'head')
- grad_values: bfloat16 [4096, 5120], P('frame', 'head')
Inputs may be any that keep to these rules, and one draw needn't show every extreme that they name: `key_lists`: row b holds 6 distinct blocks: b, the next block of the same index of frame (cyclic over its 2 blocks), and four blocks on indices of frame that differ from b's index by distinct signed powers of two. `frame_tokens`: some block is full.
All inputs are finite; a program needn't handle non-finite values.
Results may differ from a plain program's by a relative error of at most 0.011.
Values may be sent and summed in bfloat16 or wider, within the bound.
A program may use at most 192 MiB of HBM per device.

v0:
```python
import math

import jax
import jax.numpy as jnp
from jax import lax
from jax.sharding import PartitionSpec as P

HEADS = 40
HD = 128
BLK = 128


kl_weight = 1.0


def from_behind(value, axis, steps):
    count = lax.axis_size(axis)
    leading, last = (max(0, -steps), min(count, count - steps))
    return lax.ppermute(value, axis, [(source, source + steps) for source in range(leading, last)])


def local(queries, keys, values, policy_grad, ref_velocity, key_lists, frame_tokens):
    rows, cols = queries.shape
    heads_here = cols // HD
    blocks_here = rows // BLK
    list_len = key_lists.shape[1]
    all_blocks = frame_tokens.shape[0]
    scale = 1.0 / math.sqrt(HD)
    levels = lax.axis_size("frame").bit_length() - 1
    me_index = lax.axis_index("frame")
    offsets = [0]
    pool_k = [keys]
    pool_v = [values]
    for level in range(levels):
        for sign in (1, -1):
            moved = from_behind((keys, values), "frame", sign * (1 << level))
            offsets.append(-sign * (1 << level))
            pool_k.append(moved[0])
            pool_v.append(moved[1])
    classes = len(offsets)
    pool_keys = jnp.stack(pool_k).reshape(classes * blocks_here, BLK, cols)
    pool_values = jnp.stack(pool_v).reshape(classes * blocks_here, BLK, cols)
    owner_gap = key_lists // blocks_here - me_index
    class_of = jnp.zeros_like(key_lists)
    for position, offset in enumerate(offsets):
        class_of = class_of + jnp.where(owner_gap == offset, position, 0)
    pool_index = class_of * blocks_here + key_lists % blocks_here
    key_block = pool_keys[pool_index].reshape(blocks_here, list_len * BLK, heads_here, HD)
    value_block = pool_values[pool_index].reshape(blocks_here, list_len * BLK, heads_here, HD)
    counts = jnp.sum(
        jnp.where(key_lists[..., None] == jnp.arange(all_blocks, dtype=jnp.int32), frame_tokens, 0),
        axis=-1,
    )
    valid = (jnp.arange(BLK, dtype=jnp.int32)[None, None, :] < counts[..., None]).reshape(
        blocks_here, list_len * BLK
    )
    query4 = queries.reshape(blocks_here, BLK, heads_here, HD)
    scores = (
        jnp.einsum("bqhd,bkhd->bhqk", query4, key_block, preferred_element_type=jnp.float32) * scale
    )
    scores = jnp.where(valid[:, None, None, :], scores, -1e30)
    highest = jnp.max(scores, axis=-1, keepdims=True)
    expd = jnp.exp(scores - highest)
    probs = expd / jnp.sum(expd, axis=-1, keepdims=True)
    probs16 = probs.astype(jnp.bfloat16)
    attn = jnp.einsum("bhqk,bkhd->bqhd", probs16, value_block, preferred_element_type=jnp.float32)
    diff = attn - ref_velocity.reshape(blocks_here, BLK, heads_here, HD).astype(jnp.float32)
    squares = lax.psum(jnp.sum(diff * diff, axis=(2, 3)), "head")
    kl = squares / (HEADS * HD)
    upstream = (
        policy_grad.reshape(blocks_here, BLK, heads_here, HD).astype(jnp.float32)
        + kl_weight * diff / (1.0 + kl)[:, :, None, None]
    )
    grad16 = upstream.astype(jnp.bfloat16)
    grad_probs = jnp.einsum(
        "bqhd,bkhd->bhqk", grad16, value_block, preferred_element_type=jnp.float32
    )
    delta = jnp.transpose(jnp.sum(grad16.astype(jnp.float32) * attn, axis=-1), (0, 2, 1))
    grad_scores16 = (probs * (grad_probs - delta[..., None])).astype(jnp.bfloat16)
    grad_q = (
        jnp.einsum("bhqk,bkhd->bqhd", grad_scores16, key_block, preferred_element_type=jnp.float32)
        * scale
    ).astype(jnp.bfloat16)
    part_k = (
        jnp.einsum("bhqk,bqhd->bkhd", grad_scores16, query4, preferred_element_type=jnp.float32)
        * scale
    )
    part_v = jnp.einsum("bhqk,bqhd->bkhd", probs16, grad16, preferred_element_type=jnp.float32)
    part_k = part_k.reshape(blocks_here * list_len, BLK * cols)
    part_v = part_v.reshape(blocks_here * list_len, BLK * cols)
    flat_index = pool_index.reshape(-1)
    selector = (
        jnp.arange(classes * blocks_here, dtype=jnp.int32)[:, None] == flat_index[None, :]
    ).astype(jnp.float32)
    pooled_k = jnp.dot(selector, part_k, precision=lax.Precision.HIGHEST).reshape(
        classes, blocks_here, BLK * cols
    )
    pooled_v = jnp.dot(selector, part_v, precision=lax.Precision.HIGHEST).reshape(
        classes, blocks_here, BLK * cols
    )
    total_k = pooled_k[0]
    total_v = pooled_v[0]
    for position in range(1, classes):
        back = from_behind(
            (pooled_k[position].astype(jnp.bfloat16), pooled_v[position].astype(jnp.bfloat16)),
            "frame",
            offsets[position],
        )
        total_k = total_k + back[0].astype(jnp.float32)
        total_v = total_v + back[1].astype(jnp.float32)
    grad_queries = grad_q.reshape(rows, cols)
    grad_keys = total_k.reshape(rows, cols).astype(jnp.bfloat16)
    grad_values = total_v.reshape(rows, cols).astype(jnp.bfloat16)
    return (grad_queries, grad_keys, grad_values)


def solution(mesh):
    in_specs = (
        P("frame", "head"),
        P("frame", "head"),
        P("frame", "head"),
        P("frame", "head"),
        P("frame", "head"),
        P("frame", None),
        P(),
    )
    out_specs = (P("frame", "head"), P("frame", "head"), P("frame", "head"))
    return jax.shard_map(local, mesh=mesh, in_specs=in_specs, out_specs=out_specs, check_vma=False)
```

profile of v0, /device:TPU:16, one launch (start us, length us, event | category | flops | bytes accessed | tf_op | source)
XLA Modules:
  0.0 827.2 jit_solution(5974124078474056015)
XLA Ops:
  0.6 3.4 collective-permute-start
  4.0 4.2 collective-permute-start.1
  8.3 2.5 collective-permute-start.2
  10.8 4.2 collective-permute-start.3
  15.1 3.5 collective-permute-start.4
  20.1 3.6 reshape.133
  26.1 3.5 reshape.131
  30.0 3.6 reshape.132
  33.6 3.4 copy.49
  37.1 2.6 bitcast_dynamic-update-slice_fusion.17
  42.2 18.3 %collective-permute-done = bf16[256,2560]{1,0:T(8,128)(2,1)} collective-permute-done((bf16[256,2560]{1,0:T(8,128)(2,1)}, bf16[256,2560]{1,0:T(8,128)(2,1)}, u32[]{:S(2)}, u32[]{:S(2)}) %collective-permute-start) | collective-permute-done | bytes 1310752 | tf_op jit(solution)/shard_map/ppermute | solution.py:19
  66.6 2.5 bitcast_dynamic-update-slice_fusion.15
  69.1 20.4 %collective-permute-done.2 = bf16[256,2560]{1,0:T(8,128)(2,1)} collective-permute-done((bf16[256,2560]{1,0:T(8,128)(2,1)}, bf16[256,2560]{1,0:T(8,128)(2,1)}, u32[]{:S(2)}, u32[]{:S(2)}) %collective-permute-start.2) | collective-permute-done | bytes 1310752 | tf_op jit(solution)/shard_map/ppermute | solution.py:19
  94.3 7.5 collective-permute-start.8
  101.8 2.5 bitcast_dynamic-update-slice_fusion.13
  104.3 45.5 %collective-permute-start.9 = (bf16[256,2560]{1,0:T(8,128)(2,1)}, bf16[256,2560]{1,0:T(8,128)(2,1)}, u32[]{:S(2)}, u32[]{:S(2)}) collective-permute-start(bf16[256,2560]{1,0:T(8,128)(2,1)} %param.9), channel_id=1, source_target_pairs={{2,0},{4,2},{6,4},{8,6},{10,8},{12,10},{14,12},{16,14},{18,16},{20... | collective-permute-start | bytes 3932168 | tf_op jit(solution)/shard_map/ppermute | solution.py:19
  155.4 4.8 collective-permute-start.11
  161.4 5.5 collective-permute-done.7
  169.9 9.2 %gather_fusion = bf16[12,128,2560]{2,1,0:T(8,128)(2,1)} fusion(bf16[18,128,2560]{2,1,0:T(8,128)(2,1)} %bitcast.9, s32[1024]{0:T(1024)S(1)} %pad_clamp_fusion), kind=kCustom, calls=%fused_computation | custom fusion | bytes 15728688 | tf_op jit(solution)/shard_map/gather | solution.py:48
  179.2 13.9 %reshape.100 = bf16[2,768,20,128]{3,2,1,0:T(8,128)(2,1)} reshape(bf16[12,128,2560]{2,1,0:T(8,128)(2,1)} %gather_fusion) | data formatting | bytes 15728640 | tf_op jit(solution)/shard_map/reshape | solution.py:48
  193.1 12.2 %copy.53 = bf16[2,768,20,128]{1,3,2,0:T(8,128)(2,1)} copy(bf16[2,768,20,128]{3,2,1,0:T(8,128)(2,1)} %reshape.100) | data formatting | bytes 15728640 | tf_op jit(solution)/shard_map/reshape | solution.py:48
  205.3 4.7 collective-permute-done.8
  215.7 2.5 bitcast_dynamic-update-slice_fusion.6
  218.2 5.8 collective-permute-start.15
  224.0 2.5 bitcast_dynamic-update-slice_fusion.5
  226.5 8.6 %collective-permute-done.11 = bf16[256,2560]{1,0:T(8,128)(2,1)} collective-permute-done((bf16[256,2560]{1,0:T(8,128)(2,1)}, bf16[256,2560]{1,0:T(8,128)(2,1)}, u32[]{:S(2)}, u32[]{:S(2)}) %collective-permute-start.11) | collective-permute-done | bytes 1310752 | tf_op jit(solution)/shard_map/ppermute | solution.py:19
  237.6 2.5 bitcast_dynamic-update-slice_fusion.3
  240.1 51.2 %collective-permute-done.13 = bf16[256,2560]{1,0:T(8,128)(2,1)S(1)} collective-permute-done((bf16[256,2560]{1,0:T(8,128)(2,1)}, bf16[256,2560]{1,0:T(8,128)(2,1)S(1)}, u32[]{:S(2)}, u32[]{:S(2)}) %collective-permute-start.13) | collective-permute-done | bytes 1310752 | tf_op jit(solution)/shard_map/ppermute | solution.py:19
  293.7 24.2 %collective-permute-done.15 = bf16[256,2560]{1,0:T(8,128)(2,1)S(1)} collective-permute-done((bf16[256,2560]{1,0:T(8,128)(2,1)}, bf16[256,2560]{1,0:T(8,128)(2,1)S(1)}, u32[]{:S(2)}, u32[]{:S(2)}) %collective-permute-start.15) | collective-permute-done | bytes 1310752 | tf_op jit(solution)/shard_map/ppermute | solution.py:19
  319.1 9.1 %gather_fusion.1 = bf16[12,128,2560]{2,1,0:T(8,128)(2,1)} fusion(bf16[18,128,2560]{2,1,0:T(8,128)(2,1)} %bitcast.87, s32[1024]{0:T(1024)S(1)} %pad_clamp_fusion), kind=kCustom, calls=%fused_computation.1 | custom fusion | bytes 15728688 | tf_op jit(solution)/shard_map/gather | solution.py:49
  328.2 13.9 %reshape.103 = bf16[2,768,20,128]{3,2,1,0:T(8,128)(2,1)} reshape(bf16[12,128,2560]{2,1,0:T(8,128)(2,1)} %gather_fusion.1) | data formatting | bytes 15728640 | tf_op jit(solution)/shard_map/reshape | solution.py:49
  342.1 11.4 %fusion.28 = f32[2,20,768,128]{3,2,1,0:T(8,128)} fusion(bf16[2,768,20,128]{1,3,2,0:T(8,128)(2,1)} %copy.53, bf16[2,128,20,128]{3,2,1,0:T(8,128)(2,1)} %reshape.131), kind=kOutput, calls=%fused_computation.61 | convolution fusion | flops 1006632960 | bytes 24903680 | tf_op jit(solution)/shard_map/bqhd,bkhd->bhqk/dot_general | solution.py:59
  353.6 18.8 %fusion.49 = (f32[2,20,128]{2,1,0:T(8,128)S(1)}, f32[2,20,128,768]{2,3,1,0:T(8,128)}) fusion(f32[2,20,768,128]{3,2,1,0:T(8,128)} %fusion.28, pred[2,768]{1,0:T(4,128)(4,1)S(1)} %bitcast_compare_fusion), kind=kOutput, calls=%fused_computation.102 | output fusion | flops 23593728 | bytes 31479296 | tf_op jit(solution)/shard_map/sub | solution.py:63
  372.4 8.9 %fusion.8 = bf16[2,20,128,768]{2,3,1,0:T(8,128)(2,1)} fusion(f32[2,20,128,768]{2,3,1,0:T(8,128)} %get-tuple-element.30, f32[2,20,128]{2,1,0:T(8,128)S(1)} %get-tuple-element.29), kind=kLoop, calls=%fused_computation.14 | loop fusion | flops 7864320 | bytes 23613440 | tf_op jit(solution)/shard_map/convert_element_type | solution.py:65
  381.3 10.4 %multiply_reduce_fusion = (f32[2,128]{1,0:T(2,128)S(1)}, f32[2,20,128,128]{3,2,1,0:T(8,128)}) fusion(f32[2,128,20,128]{1,3,2,0:T(8,128)S(1)} %copy.48, bf16[2,20,128,768]{2,3,1,0:T(8,128)(2,1)} %fusion.8, bf16[2,768,20,128]{3,2,1,0:T(8,128)(2,1)} %reshape.103), kind=kOutput, calls=%fused_computation.39 | convolution fusion | flops 1008598784 | bytes 20972544 | tf_op jit(solution)/shard_map/bhqk,bkhd->bqhd/dot_general | solution.py:66
  394.1 3.7 fusion.25
  398.9 7.7 convolution_bitcast_fusion
  406.6 13.7 %multiply_convert_fusion = bf16[2,20,128,768]{2,3,1,0:T(8,128)(2,1)} fusion(f32[2,20,128]{2,1,0:T(8,128)S(1)} %bitcast.90, f32[2,20,128,768]{2,3,1,0:T(8,128)} %get-tuple-element.30, f32[2,20,128]{2,1,0:T(8,128)S(1)} %get-tuple-element.29, bf16[2,128,20,128]{1,3,2,0:T(8,128)(2,1)S(1)} %get-tuple-element.10, bf16[2,768,20,128]{3,2,1,0:T(8,128)(2,1)} %reshape.103), kind=kOutput, calls=%fused_computation.8 | convolution fusion | flops 1022361600 | bytes 32808960 | tf_op jit(solution)/shard_map/bqhd,bkhd->bhqk/dot_general | solution.py:75
  420.3 4.5 multiply_bitcast_fusion
  424.8 24.4 %copy.57 = f32[2,768,20,128]{3,2,1,0:T(8,128)} copy(f32[2,768,20,128]{3,1,2,0:T(8,128)S(1)} %multiply_bitcast_fusion) | data formatting | bytes 31457280 | tf_op jit(solution)/shard_map/mul | solution.py:85
  449.2 19.3 %reshape.105 = f32[12,327680]{1,0:T(8,128)} reshape(f32[2,768,20,128]{3,2,1,0:T(8,128)} %copy.57) | data formatting | bytes 31457280 | tf_op jit(solution)/shard_map/reshape | solution.py:89
  468.5 25.8 %fusion.50 = (bf16[18,327680]{1,0:T(8,128)(2,1)}, f32[18,327680]{1,0:T(8,128)}) fusion(f32[12,327680]{1,0:T(8,128)} %reshape.105, s32[12]{0:T(128)S(1)} %eq.67), kind=kOutput, calls=%fused_computation.103 | convolution fusion | flops 855245056 | bytes 51118128 | tf_op jit(solution)/shard_map/dot_general | solution.py:95
  494.4 24.5 %fusion.48 = (bf16[2,327680]{1,0:T(2,128)(2,1)}, bf16[2,327680]{1,0:T(2,128)(2,1)}, bf16[2,327680]{1,0:T(2,128)(2,1)}, bf16[2,327680]{1,0:T(2,128)(2,1)}, bf16[2...) fusion(bf16[18,327680]{1,0:T(8,128)(2,1)} %get-tuple-element.33), kind=kLoop, calls=%fused_computation.101 | loop fusion | bytes 20971520 | tf_op jit(solution)/shard_map/slice | solution.py:105
  520.2 7.5 collective-permute-start.22
  529.6 3.9 collective-permute-start.20
  535.5 17.8 %copy.59 = f32[2,768,20,128]{3,2,1,0:T(8,128)} copy(f32[2,768,20,128]{1,3,2,0:T(8,128)} %convolution_bitcast_fusion) | data formatting | bytes 31457280 | tf_op jit(solution)/shard_map/bhqk,bqhd->bkhd/transpose | solution.py:88
  553.3 19.3 %reshape.106 = f32[12,327680]{1,0:T(8,128)} reshape(f32[2,768,20,128]{3,2,1,0:T(8,128)} %copy.59) | data formatting | bytes 31457280 | tf_op jit(solution)/shard_map/reshape | solution.py:90
  572.6 25.7 %fusion.51 = (bf16[18,327680]{1,0:T(8,128)(2,1)}, f32[18,327680]{1,0:T(8,128)}) fusion(f32[12,327680]{1,0:T(8,128)} %reshape.106, s32[12]{0:T(128)S(1)} %eq.67), kind=kOutput, calls=%fused_computation.104 | convolution fusion | flops 855245056 | bytes 51118128 | tf_op jit(solution)/shard_map/dot_general | solution.py:98
  598.3 4.8 collective-permute-start.18
  603.1 25.7 %fusion.47 = (bf16[2,327680]{1,0:T(2,128)(2,1)}, bf16[2,327680]{1,0:T(2,128)(2,1)}, bf16[2,327680]{1,0:T(2,128)(2,1)}, bf16[2,327680]{1,0:T(2,128)(2,1)}, bf16[2...) fusion(bf16[18,327680]{1,0:T(8,128)(2,1)} %get-tuple-element.35), kind=kLoop, calls=%fused_computation.100 | loop fusion | bytes 20971520 | tf_op jit(solution)/shard_map/slice | solution.py:105
  628.8 4.0 collective-permute-start.17
  632.8 3.6 collective-permute-start.16
  637.8 7.6 collective-permute-start.30
  645.4 3.5 collective-permute-start.29
  648.9 7.7 fusion.26
  658.8 33.9 %collective-permute-done.17 = bf16[2,327680]{1,0:T(2,128)(2,1)} collective-permute-done((bf16[2,327680]{1,0:T(2,128)(2,1)}, bf16[2,327680]{1,0:T(2,128)(2,1)}, u32[]{:S(2)}, u32[]{:S(2)}) %collective-permute-start.17) | collective-permute-done | bytes 1310752 | tf_op jit(solution)/shard_map/ppermute | solution.py:19
  696.5 4.8 collective-permute-start.26
  701.4 20.9 %collective-permute-done.30 = bf16[2,327680]{1,0:T(2,128)(2,1)} collective-permute-done((bf16[2,327680]{1,0:T(2,128)(2,1)}, bf16[2,327680]{1,0:T(2,128)(2,1)}, u32[]{:S(2)}, u32[]{:S(2)}) %collective-permute-start.30) | collective-permute-done | bytes 1310752 | tf_op jit(solution)/shard_map/ppermute | solution.py:19
  722.2 2.5 collective-permute-start.25
  724.8 25.6 %collective-permute-start.24 = (bf16[2,327680]{1,0:T(2,128)(2,1)}, bf16[2,327680]{1,0:T(2,128)(2,1)}, u32[]{:S(2)}, u32[]{:S(2)}) collective-permute-start(bf16[2,327680]{1,0:T(2,128)(2,1)} %get-tuple-element.13), channel_id=1, source_target_pairs={{2,0},{4,2},{6,4},{8,6},{10,8},{12,10},{14,12},{16,14},{18,16},{20... | collective-permute-start | bytes 3932168 | tf_op jit(solution)/shard_map/ppermute | solution.py:19
  750.4 9.8 %add_convert_fusion.1 = bf16[2,327680]{1,0:T(2,128)(2,1)S(1)} fusion(bf16[2,327680]{1,0:T(2,128)(2,1)} %collective-permute-done.23, bf16[2,327680]{1,0:T(2,128)(2,1)} %collective-permute-done.22, bf16[2,327680]{1,0:T(2,128)(2,1)} %collective-permute-done.21, bf16[2,327680]{1,0:T(2,128)(2,1)} %collective-permute-done.20, ...), kind=kLoop, calls=%fused_computation.36 | loop fusion | flops 11141120 | bytes 14417920 | tf_op jit(solution)/shard_map/convert_element_type | solution.py:112
  762.5 13.7 %collective-permute-done.27 = bf16[2,327680]{1,0:T(2,128)(2,1)} collective-permute-done((bf16[2,327680]{1,0:T(2,128)(2,1)}, bf16[2,327680]{1,0:T(2,128)(2,1)}, u32[]{:S(2)}, u32[]{:S(2)}) %collective-permute-start.27) | collective-permute-done | bytes 1310752 | tf_op jit(solution)/shard_map/ppermute | solution.py:19
  778.5 36.2 %collective-permute-done.25 = bf16[2,327680]{1,0:T(2,128)(2,1)} collective-permute-done((bf16[2,327680]{1,0:T(2,128)(2,1)}, bf16[2,327680]{1,0:T(2,128)(2,1)}, u32[]{:S(2)}, u32[]{:S(2)}) %collective-permute-start.25) | collective-permute-done | bytes 1310752 | tf_op jit(solution)/shard_map/ppermute | solution.py:19
  814.7 9.8 %add_convert_fusion = bf16[2,327680]{1,0:T(2,128)(2,1)S(1)} fusion(bf16[2,327680]{1,0:T(2,128)(2,1)} %collective-permute-done.31, bf16[2,327680]{1,0:T(2,128)(2,1)} %collective-permute-done.30, bf16[2,327680]{1,0:T(2,128)(2,1)} %collective-permute-done.29, bf16[2,327680]{1,0:T(2,128)(2,1)S(1)} %collective-permute-done.28, ...), kind=kLoop, calls=%fused_computation.35 | loop fusion | flops 11141120 | bytes 14417920 | tf_op jit(solution)/shard_map/convert_element_type | solution.py:113
  (75 shorter events, 62.2 us)
Async XLA Ops:
  0.6 59.8 %collective-permute-start = (bf16[256,2560]{1,0:T(8,128)(2,1)}, bf16[256,2560]{1,0:T(8,128)(2,1)}, u32[]{:S(2)}, u32[]{:S(2)}) collective-permute-start(bf16[256,2560]{1,0:T(8,128)(2,1)} %param.8), channel_id=1, source_target_pairs={{0,2},{2,4},{4,6},{6,8},{8,10},{10,12},{12,14},{14,16},{16,18},{18... | collective-permute-start | bytes 3932168 | tf_op jit(solution)/shard_map/ppermute | solution.py:19
  4.0 61.2 %collective-permute-start.1 = (bf16[256,2560]{1,0:T(8,128)(2,1)}, bf16[256,2560]{1,0:T(8,128)(2,1)}, u32[]{:S(2)}, u32[]{:S(2)}) collective-permute-start(bf16[256,2560]{1,0:T(8,128)(2,1)} %param.8), channel_id=1, source_target_pairs={{2,0},{4,2},{6,4},{8,6},{10,8},{12,10},{14,12},{16,14},{18,16},{20... | collective-permute-start | bytes 3932168 | tf_op jit(solution)/shard_map/ppermute | solution.py:19
  8.3 81.2 %collective-permute-start.2 = (bf16[256,2560]{1,0:T(8,128)(2,1)}, bf16[256,2560]{1,0:T(8,128)(2,1)}, u32[]{:S(2)}, u32[]{:S(2)}) collective-permute-start(bf16[256,2560]{1,0:T(8,128)(2,1)} %param.8), channel_id=1, source_target_pairs={{0,4},{2,6},{4,8},{6,10},{8,12},{10,14},{12,16},{14,18},{16,20},{1... | collective-permute-start | bytes 3932168 | tf_op jit(solution)/shard_map/ppermute | solution.py:19
  10.8 83.4 %collective-permute-start.3 = (bf16[256,2560]{1,0:T(8,128)(2,1)}, bf16[256,2560]{1,0:T(8,128)(2,1)}, u32[]{:S(2)}, u32[]{:S(2)}) collective-permute-start(bf16[256,2560]{1,0:T(8,128)(2,1)} %param.8), channel_id=1, source_target_pairs={{4,0},{6,2},{8,4},{10,6},{12,8},{14,10},{16,12},{18,14},{20,16},{2... | collective-permute-start | bytes 3932168 | tf_op jit(solution)/shard_map/ppermute | solution.py:19
  15.1 89.2 %collective-permute-start.4 = (bf16[256,2560]{1,0:T(8,128)(2,1)}, bf16[256,2560]{1,0:T(8,128)(2,1)}, u32[]{:S(2)}, u32[]{:S(2)}) collective-permute-start(bf16[256,2560]{1,0:T(8,128)(2,1)} %param.8), channel_id=1, source_target_pairs={{0,8},{2,10},{4,12},{6,14},{8,16},{10,18},{12,20},{14,22},{16,24},... | collective-permute-start | bytes 3932168 | tf_op jit(solution)/shard_map/ppermute | solution.py:19
  26.0 3.5 copy-start.5
  37.1 23.4 %copy-start.4 = (bf16[256,2560]{1,0:T(8,128)(2,1)S(1)}, bf16[256,2560]{1,0:T(8,128)(2,1)}, u32[]{:S(2)}) copy-start(bf16[256,2560]{1,0:T(8,128)(2,1)} %param.8) | copy-start | bytes 3932164
  60.5 91.8 %collective-permute-start.5 = (bf16[256,2560]{1,0:T(8,128)(2,1)S(1)}, bf16[256,2560]{1,0:T(8,128)(2,1)S(1)}, u32[]{:S(2)}, u32[]{:S(2)}) collective-permute-start(bf16[256,2560]{1,0:T(8,128)(2,1)S(1)} %copy-done.4), channel_id=1, source_target_pairs={{8,0},{10,2},{12,4},{14,6},{16,8},{18,10},{20,12},{22,14},{24,16},... | collective-permute-start | bytes 3932168 | tf_op jit(solution)/shard_map/ppermute | solution.py:19
  65.3 90.1 %collective-permute-start.6 = (bf16[256,2560]{1,0:T(8,128)(2,1)S(1)}, bf16[256,2560]{1,0:T(8,128)(2,1)S(1)}, u32[]{:S(2)}, u32[]{:S(2)}) collective-permute-start(bf16[256,2560]{1,0:T(8,128)(2,1)S(1)} %copy-done.4), channel_id=1, source_target_pairs={{0,16},{2,18},{4,20},{6,22},{8,24},{10,26},{12,28},{14,30},{1,17},... | collective-permute-start | bytes 3932168 | tf_op jit(solution)/shard_map/ppermute | solution.py:19
  89.5 77.4 %collective-permute-start.7 = (bf16[256,2560]{1,0:T(8,128)(2,1)S(1)}, bf16[256,2560]{1,0:T(8,128)(2,1)S(1)}, u32[]{:S(2)}, u32[]{:S(2)}) collective-permute-start(bf16[256,2560]{1,0:T(8,128)(2,1)S(1)} %copy-done.4), channel_id=1, source_target_pairs={{16,0},{18,2},{20,4},{22,6},{24,8},{26,10},{28,12},{30,14},{17,1},... | collective-permute-start | bytes 3932168 | tf_op jit(solution)/shard_map/ppermute | solution.py:19
  94.3 115.8 %collective-permute-start.8 = (bf16[256,2560]{1,0:T(8,128)(2,1)}, bf16[256,2560]{1,0:T(8,128)(2,1)}, u32[]{:S(2)}, u32[]{:S(2)}) collective-permute-start(bf16[256,2560]{1,0:T(8,128)(2,1)} %param.9), channel_id=1, source_target_pairs={{0,2},{2,4},{4,6},{6,8},{8,10},{10,12},{12,14},{14,16},{16,18},{18... | collective-permute-start | bytes 3932168 | tf_op jit(solution)/shard_map/ppermute | solution.py:19
  104.3 110.1 %collective-permute-start.9 = (bf16[256,2560]{1,0:T(8,128)(2,1)}, bf16[256,2560]{1,0:T(8,128)(2,1)}, u32[]{:S(2)}, u32[]{:S(2)}) collective-permute-start(bf16[256,2560]{1,0:T(8,128)(2,1)} %param.9), channel_id=1, source_target_pairs={{2,0},{4,2},{6,4},{8,6},{10,8},{12,10},{14,12},{16,14},{18,16},{20... | collective-permute-start | bytes 3932168 | tf_op jit(solution)/shard_map/ppermute | solution.py:19
  152.3 65.9 %collective-permute-start.10 = (bf16[256,2560]{1,0:T(8,128)(2,1)}, bf16[256,2560]{1,0:T(8,128)(2,1)}, u32[]{:S(2)}, u32[]{:S(2)}) collective-permute-start(bf16[256,2560]{1,0:T(8,128)(2,1)} %param.9), channel_id=1, source_target_pairs={{0,4},{2,6},{4,8},{6,10},{8,12},{10,14},{12,16},{14,18},{16,20},{1... | collective-permute-start | bytes 3932168 | tf_op jit(solution)/shard_map/ppermute | solution.py:19
  155.4 79.7 %collective-permute-start.11 = (bf16[256,2560]{1,0:T(8,128)(2,1)}, bf16[256,2560]{1,0:T(8,128)(2,1)}, u32[]{:S(2)}, u32[]{:S(2)}) collective-permute-start(bf16[256,2560]{1,0:T(8,128)(2,1)} %param.9), channel_id=1, source_target_pairs={{4,0},{6,2},{8,4},{10,6},{12,8},{14,10},{16,12},{18,14},{20,16},{2... | collective-permute-start | bytes 3932168 | tf_op jit(solution)/shard_map/ppermute | solution.py:19
  166.8 70.7 %collective-permute-start.12 = (bf16[256,2560]{1,0:T(8,128)(2,1)}, bf16[256,2560]{1,0:T(8,128)(2,1)}, u32[]{:S(2)}, u32[]{:S(2)}) collective-permute-start(bf16[256,2560]{1,0:T(8,128)(2,1)} %param.9), channel_id=1, source_target_pairs={{0,8},{2,10},{4,12},{6,14},{8,16},{10,18},{12,20},{14,22},{16,24},... | collective-permute-start | bytes 3932168 | tf_op jit(solution)/shard_map/ppermute | solution.py:19
  210.0 81.2 %collective-permute-start.13 = (bf16[256,2560]{1,0:T(8,128)(2,1)}, bf16[256,2560]{1,0:T(8,128)(2,1)S(1)}, u32[]{:S(2)}, u32[]{:S(2)}) collective-permute-start(bf16[256,2560]{1,0:T(8,128)(2,1)} %param.9), channel_id=1, source_target_pairs={{8,0},{10,2},{12,4},{14,6},{16,8},{18,10},{20,12},{22,14},{24,16},... | collective-permute-start | bytes 3932168 | tf_op jit(solution)/shard_map/ppermute | solution.py:19
  214.4 78.1 %collective-permute-start.14 = (bf16[256,2560]{1,0:T(8,128)(2,1)}, bf16[256,2560]{1,0:T(8,128)(2,1)S(1)}, u32[]{:S(2)}, u32[]{:S(2)}) collective-permute-start(bf16[256,2560]{1,0:T(8,128)(2,1)} %param.9), channel_id=1, source_target_pairs={{0,16},{2,18},{4,20},{6,22},{8,24},{10,26},{12,28},{14,30},{1,17},... | collective-permute-start | bytes 3932168 | tf_op jit(solution)/shard_map/ppermute | solution.py:19
  218.2 99.7 %collective-permute-start.15 = (bf16[256,2560]{1,0:T(8,128)(2,1)}, bf16[256,2560]{1,0:T(8,128)(2,1)S(1)}, u32[]{:S(2)}, u32[]{:S(2)}) collective-permute-start(bf16[256,2560]{1,0:T(8,128)(2,1)} %param.9), channel_id=1, source_target_pairs={{16,0},{18,2},{20,4},{22,6},{24,8},{26,10},{28,12},{30,14},{17,1},... | collective-permute-start | bytes 3932168 | tf_op jit(solution)/shard_map/ppermute | solution.py:19
  394.1 4.8 copy-start
  406.6 13.7 %copy-start.1 = (bf16[2,128,20,128]{3,2,1,0:T(8,128)(2,1)S(1)}, bf16[2,128,20,128]{3,2,1,0:T(8,128)(2,1)}, u32[]{:S(2)}) copy-start(bf16[2,128,20,128]{3,2,1,0:T(8,128)(2,1)} %reshape.131) | copy-start | bytes 3932164
  518.9 79.4 %collective-permute-start.23 = (bf16[2,327680]{1,0:T(2,128)(2,1)}, bf16[2,327680]{1,0:T(2,128)(2,1)}, u32[]{:S(2)}, u32[]{:S(2)}) collective-permute-start(bf16[2,327680]{1,0:T(2,128)(2,1)} %get-tuple-element.22), channel_id=1, source_target_pairs={{0,16},{2,18},{4,20},{6,22},{8,24},{10,26},{12,28},{14,30},{1,17},... | collective-permute-start | bytes 3932168 | tf_op jit(solution)/shard_map/ppermute | solution.py:19
  520.2 108.6 %collective-permute-start.22 = (bf16[2,327680]{1,0:T(2,128)(2,1)}, bf16[2,327680]{1,0:T(2,128)(2,1)}, u32[]{:S(2)}, u32[]{:S(2)}) collective-permute-start(bf16[2,327680]{1,0:T(2,128)(2,1)} %get-tuple-element.23), channel_id=1, source_target_pairs={{16,0},{18,2},{20,4},{22,6},{24,8},{26,10},{28,12},{30,14},{17,1},... | collective-permute-start | bytes 3932168 | tf_op jit(solution)/shard_map/ppermute | solution.py:19
  527.7 105.1 %collective-permute-start.21 = (bf16[2,327680]{1,0:T(2,128)(2,1)}, bf16[2,327680]{1,0:T(2,128)(2,1)}, u32[]{:S(2)}, u32[]{:S(2)}) collective-permute-start(bf16[2,327680]{1,0:T(2,128)(2,1)} %get-tuple-element.24), channel_id=1, source_target_pairs={{0,8},{2,10},{4,12},{6,14},{8,16},{10,18},{12,20},{14,22},{16,24},... | collective-permute-start | bytes 3932168 | tf_op jit(solution)/shard_map/ppermute | solution.py:19
  529.6 106.9 %collective-permute-start.20 = (bf16[2,327680]{1,0:T(2,128)(2,1)}, bf16[2,327680]{1,0:T(2,128)(2,1)}, u32[]{:S(2)}, u32[]{:S(2)}) collective-permute-start(bf16[2,327680]{1,0:T(2,128)(2,1)} %get-tuple-element.25), channel_id=1, source_target_pairs={{8,0},{10,2},{12,4},{14,6},{16,8},{18,10},{20,12},{22,14},{24,16},... | collective-permute-start | bytes 3932168 | tf_op jit(solution)/shard_map/ppermute | solution.py:19
  533.6 104.2 %collective-permute-start.19 = (bf16[2,327680]{1,0:T(2,128)(2,1)S(1)}, bf16[2,327680]{1,0:T(2,128)(2,1)}, u32[]{:S(2)}, u32[]{:S(2)}) collective-permute-start(bf16[2,327680]{1,0:T(2,128)(2,1)S(1)} %get-tuple-element.26), channel_id=1, source_target_pairs={{0,4},{2,6},{4,8},{6,10},{8,12},{10,14},{12,16},{14,18},{16,20},{1... | collective-permute-start | bytes 3932168 | tf_op jit(solution)/shard_map/ppermute | solution.py:19
  598.3 47.1 %collective-permute-start.18 = (bf16[2,327680]{1,0:T(2,128)(2,1)S(1)}, bf16[2,327680]{1,0:T(2,128)(2,1)S(1)}, u32[]{:S(2)}, u32[]{:S(2)}) collective-permute-start(bf16[2,327680]{1,0:T(2,128)(2,1)S(1)} %get-tuple-element.27), channel_id=1, source_target_pairs={{4,0},{6,2},{8,4},{10,6},{12,8},{14,10},{16,12},{18,14},{20,16},{2... | collective-permute-start | bytes 3932168 | tf_op jit(solution)/shard_map/ppermute | solution.py:19
  628.8 63.9 %collective-permute-start.17 = (bf16[2,327680]{1,0:T(2,128)(2,1)}, bf16[2,327680]{1,0:T(2,128)(2,1)}, u32[]{:S(2)}, u32[]{:S(2)}) collective-permute-start(bf16[2,327680]{1,0:T(2,128)(2,1)} %get-tuple-element.28), channel_id=1, source_target_pairs={{0,2},{2,4},{4,6},{6,8},{8,10},{10,12},{12,14},{14,16},{16,18},{18... | collective-permute-start | bytes 3932168 | tf_op jit(solution)/shard_map/ppermute | solution.py:19
  632.8 61.8 %collective-permute-start.16 = (bf16[2,327680]{1,0:T(2,128)(2,1)}, bf16[2,327680]{1,0:T(2,128)(2,1)}, u32[]{:S(2)}, u32[]{:S(2)}) collective-permute-start(bf16[2,327680]{1,0:T(2,128)(2,1)} %get-tuple-element.21), channel_id=1, source_target_pairs={{2,0},{4,2},{6,4},{8,6},{10,8},{12,10},{14,12},{16,14},{18,16},{20... | collective-permute-start | bytes 3932168 | tf_op jit(solution)/shard_map/ppermute | solution.py:19
  636.5 60.0 %collective-permute-start.31 = (bf16[2,327680]{1,0:T(2,128)(2,1)}, bf16[2,327680]{1,0:T(2,128)(2,1)}, u32[]{:S(2)}, u32[]{:S(2)}) collective-permute-start(bf16[2,327680]{1,0:T(2,128)(2,1)} %get-tuple-element.14), channel_id=1, source_target_pairs={{0,16},{2,18},{4,20},{6,22},{8,24},{10,26},{12,28},{14,30},{1,17},... | collective-permute-start | bytes 3932168 | tf_op jit(solution)/shard_map/ppermute | solution.py:19
  637.8 84.4 %collective-permute-start.30 = (bf16[2,327680]{1,0:T(2,128)(2,1)}, bf16[2,327680]{1,0:T(2,128)(2,1)}, u32[]{:S(2)}, u32[]{:S(2)}) collective-permute-start(bf16[2,327680]{1,0:T(2,128)(2,1)} %get-tuple-element.15), channel_id=1, source_target_pairs={{16,0},{18,2},{20,4},{22,6},{24,8},{26,10},{28,12},{30,14},{17,1},... | collective-permute-start | bytes 3932168 | tf_op jit(solution)/shard_map/ppermute | solution.py:19
  645.4 3.5 copy-start.2
  645.4 79.4 %collective-permute-start.29 = (bf16[2,327680]{1,0:T(2,128)(2,1)}, bf16[2,327680]{1,0:T(2,128)(2,1)}, u32[]{:S(2)}, u32[]{:S(2)}) collective-permute-start(bf16[2,327680]{1,0:T(2,128)(2,1)} %get-tuple-element.16), channel_id=1, source_target_pairs={{0,8},{2,10},{4,12},{6,14},{8,16},{10,18},{12,20},{14,22},{16,24},... | collective-permute-start | bytes 3932168 | tf_op jit(solution)/shard_map/ppermute | solution.py:19
  657.6 92.8 %copy-start.3 = (bf16[2,327680]{1,0:T(2,128)(2,1)S(1)}, bf16[2,327680]{1,0:T(2,128)(2,1)}, u32[]{:S(2)}) copy-start(bf16[2,327680]{1,0:T(2,128)(2,1)} %copy-done.2) | copy-start | bytes 3932164
  692.7 69.8 %collective-permute-start.28 = (bf16[2,327680]{1,0:T(2,128)(2,1)}, bf16[2,327680]{1,0:T(2,128)(2,1)S(1)}, u32[]{:S(2)}, u32[]{:S(2)}) collective-permute-start(bf16[2,327680]{1,0:T(2,128)(2,1)} %get-tuple-element.17), channel_id=1, source_target_pairs={{8,0},{10,2},{12,4},{14,6},{16,8},{18,10},{20,12},{22,14},{24,16},... | collective-permute-start | bytes 3932168 | tf_op jit(solution)/shard_map/ppermute | solution.py:19
  694.6 81.6 %collective-permute-start.27 = (bf16[2,327680]{1,0:T(2,128)(2,1)}, bf16[2,327680]{1,0:T(2,128)(2,1)}, u32[]{:S(2)}, u32[]{:S(2)}) collective-permute-start(bf16[2,327680]{1,0:T(2,128)(2,1)} %get-tuple-element.18), channel_id=1, source_target_pairs={{0,4},{2,6},{4,8},{6,10},{8,12},{10,14},{12,16},{14,18},{16,20},{1... | collective-permute-start | bytes 3932168 | tf_op jit(solution)/shard_map/ppermute | solution.py:19
  696.5 81.9 %collective-permute-start.26 = (bf16[2,327680]{1,0:T(2,128)(2,1)}, bf16[2,327680]{1,0:T(2,128)(2,1)}, u32[]{:S(2)}, u32[]{:S(2)}) collective-permute-start(bf16[2,327680]{1,0:T(2,128)(2,1)} %get-tuple-element.19), channel_id=1, source_target_pairs={{4,0},{6,2},{8,4},{10,6},{12,8},{14,10},{16,12},{18,14},{20,16},{2... | collective-permute-start | bytes 3932168 | tf_op jit(solution)/shard_map/ppermute | solution.py:19
  722.2 92.4 %collective-permute-start.25 = (bf16[2,327680]{1,0:T(2,128)(2,1)}, bf16[2,327680]{1,0:T(2,128)(2,1)}, u32[]{:S(2)}, u32[]{:S(2)}) collective-permute-start(bf16[2,327680]{1,0:T(2,128)(2,1)} %get-tuple-element.20), channel_id=1, source_target_pairs={{0,2},{2,4},{4,6},{6,8},{8,10},{10,12},{12,14},{14,16},{16,18},{18... | collective-permute-start | bytes 3932168 | tf_op jit(solution)/shard_map/ppermute | solution.py:19
  724.8 89.9 %collective-permute-start.24 = (bf16[2,327680]{1,0:T(2,128)(2,1)}, bf16[2,327680]{1,0:T(2,128)(2,1)}, u32[]{:S(2)}, u32[]{:S(2)}) collective-permute-start(bf16[2,327680]{1,0:T(2,128)(2,1)} %get-tuple-element.13), channel_id=1, source_target_pairs={{2,0},{4,2},{6,4},{8,6},{10,8},{12,10},{14,12},{16,14},{18,16},{20... | collective-permute-start | bytes 3932168 | tf_op jit(solution)/shard_map/ppermute | solution.py:19
where the time goes:
time: 836 us; the launch traced here: 827 us
  local copies, waits for them, and re-layouts  252 us (30%)
  waiting for transfers between devices  240 us (29%)
  starting transfers between devices  173 us (21%)
  matrix products  107 us (13%)
  other arithmetic  51.9 us (6%)
    ppermute x32, waiting for transfers between devices, from_behind(): lax.ppermute(value, axis, [(source, source + steps) for source in range(l...  240 us
    ppermute x32, starting transfers between devices, from_behind(): lax.ppermute(value, axis, [(source, source + steps) for source in range(l...  173 us
    unnamed x32, local copies, waits for them, and re-layouts  38.8 us
    reshape x2, local copies, waits for them, and re-layouts, local(): pool_keys[pool_index].reshape(blocks_here, list_len * BLK, heads_here, HD)  26.1 us
    dot_general x1, matrix products, local(): jnp.dot(selector, part_k, precision=lax.Precision.HIGHEST)  25.8 us
    slice x1, local copies, waits for them, and re-layouts, local(): pooled_v[position].astype(jnp.bfloat16)  25.7 us
    dot_general x1, matrix products, local(): jnp.dot(selector, part_v, precision=lax.Precision.HIGHEST)  25.7 us
    slice x1, local copies, waits for them, and re-layouts, local(): pooled_k[position].astype(jnp.bfloat16)  24.5 us
  transfers between devices with their start and end apart: 32, of which 12 were waited for; matrix products, arithmetic and copies ran while one was open for 24% of the time, Pallas kernels for 0%

commit v1 on v0

v1 whole, which is shorter than its diff:
```python
import functools
import math

import jax
import jax.numpy as jnp
from jax import lax
from jax.experimental import pallas as pl
from jax.experimental.pallas import tpu as pltpu
from jax.sharding import PartitionSpec as P

HD = 128
BLK = 128
KL_WEIGHT = 1.0
VMEM = 40 * 1024 * 1024

NT = (((1,), (1,)), ((), ()))
NN = (((1,), (0,)), ((), ()))
TN = (((0,), (0,)), ((), ()))


def dot(a, b, dims):
    return lax.dot_general(a, b, dims, preferred_element_type=jnp.float32)


def fetch(pool, held, sems, head, slot):
    cols = pl.ds(pl.multiple_of(head * HD, HD), HD)
    return [
        pltpu.make_async_copy(ref.at[:, cols], held.at[slot, n], sems.at[slot, n])
        for n, ref in enumerate(pool)
    ]


def rotate_in(pool, held, sems, head, heads):
    slot = lax.rem(head, 2)

    @pl.when(head == 0)
    def _():
        for copy in fetch(pool, held, sems, head, slot):
            copy.start()

    @pl.when(head + 1 < heads)
    def _():
        for copy in fetch(pool, held, sems, head + 1, 1 - slot):
            copy.start()

    for copy in fetch(pool, held, sems, head, slot):
        copy.wait()
    return slot


def listed(held, slot, where_ref, first, list_len, rows, part):
    out = []
    for n in range(list_len):
        code = where_ref[first + n]
        start = pl.multiple_of(lax.rem(code, rows // BLK) * BLK + part * rows, BLK)
        out.append(held[slot, lax.div(code, rows // BLK), pl.ds(start, BLK), :])
    return jnp.concatenate(out, axis=0)


def forward_kernel(n_pool, blocks, list_len, heads, where_ref, count_ref, q_ref, ref_ref, *rest):
    pool, (attn_ref, probs_ref, sq_ref, held, sems) = rest[:n_pool], rest[n_pool:]
    head = pl.program_id(0)
    rows = blocks * BLK
    slot = rotate_in(pool, held, sems, head, heads)
    scale = 1.0 / math.sqrt(HD)
    lane = lax.broadcasted_iota(jnp.int32, (BLK, BLK), 1)

    @pl.when(head == 0)
    def _():
        sq_ref[...] = jnp.zeros_like(sq_ref)

    for b in range(blocks):
        mine = pl.ds(b * BLK, BLK)
        k = listed(held, slot, where_ref, b * list_len, list_len, rows, 0)
        v = listed(held, slot, where_ref, b * list_len, list_len, rows, 1)
        s = dot(q_ref[mine, :], k, NT) * scale
        s = jnp.concatenate(
            [
                jnp.where(
                    lane < count_ref[b * list_len + n], s[:, n * BLK : (n + 1) * BLK], -1e30
                )
                for n in range(list_len)
            ],
            axis=1,
        )
        e = jnp.exp(s - jnp.max(s, axis=-1, keepdims=True))
        p = e * (1.0 / jnp.sum(e, axis=-1, keepdims=True))
        p16 = p.astype(jnp.bfloat16)
        probs_ref[0, mine, :] = p16
        attn = dot(p16, v, NN)
        attn_ref[mine, :] = attn
        diff = attn - ref_ref[mine, :].astype(jnp.float32)
        sq_ref[mine, :] += diff * diff


def backward_kernel(
    n_pool, blocks, list_len, heads, where_ref, q_ref, pg_ref, ref_ref, attn_ref, probs_ref, inv_ref, *rest
):
    pool, dq_ref, outs = rest[:n_pool], rest[n_pool], rest[n_pool + 1 : 2 * n_pool + 1]
    held, sems, part, out_sems = rest[2 * n_pool + 1 :]
    head = pl.program_id(0)
    rows = blocks * BLK
    slot = rotate_in(pool, held, sems, head, heads)
    scale = 1.0 / math.sqrt(HD)

    def leave(which, at):
        cols = pl.ds(pl.multiple_of(which * HD, HD), HD)
        return [
            pltpu.make_async_copy(part.at[at, n], ref.at[:, cols], out_sems.at[at, n])
            for n, ref in enumerate(outs)
        ]

    @pl.when(head >= 2)
    def _():
        for copy in leave(head - 2, slot):
            copy.wait()

    part[slot] = jnp.zeros(part.shape[1:], part.dtype)
    for b in range(blocks):
        mine = pl.ds(b * BLK, BLK)
        k = listed(held, slot, where_ref, b * list_len, list_len, rows, 0)
        v = listed(held, slot, where_ref, b * list_len, list_len, rows, 1)
        attn = attn_ref[mine, :]
        q = q_ref[mine, :]
        p16 = probs_ref[0, mine, :]
        diff = attn - ref_ref[mine, :].astype(jnp.float32)
        g16 = (pg_ref[mine, :].astype(jnp.float32) + KL_WEIGHT * diff * inv_ref[mine, :]).astype(
            jnp.bfloat16
        )
        delta = jnp.sum(g16.astype(jnp.float32) * attn, axis=-1, keepdims=True)
        ds16 = (p16.astype(jnp.float32) * (dot(g16, v, NT) - delta)).astype(jnp.bfloat16)
        dq_ref[mine, :] = (dot(ds16, k, NN) * scale).astype(jnp.bfloat16)
        dk = dot(ds16, q, TN) * scale
        dv = dot(p16, g16, TN)
        for n in range(list_len):
            code = where_ref[b * list_len + n]
            at, within = lax.div(code, blocks), lax.rem(code, blocks)
            for kind, value in ((0, dk), (1, dv)):
                start = pl.multiple_of(within * BLK + kind * rows, BLK)
                piece = value[n * BLK : (n + 1) * BLK, :]
                if b > 0:
                    piece = piece + part[slot, at, pl.ds(start, BLK), :].astype(jnp.float32)
                part[slot, at, pl.ds(start, BLK), :] = piece.astype(jnp.bfloat16)

    for copy in leave(head, slot):
        copy.start()

    @pl.when(head == heads - 1)
    def _():
        if heads > 1:
            for copy in leave(head - 1, 1 - slot):
                copy.wait()
        for copy in leave(head, slot):
            copy.wait()


def forward(where, counts, queries, ref, pool, first, heads, blocks, list_len):
    rows, keys = blocks * BLK, list_len * BLK
    n_pool = len(pool)
    column = pl.BlockSpec((rows, HD), lambda h, *_: (0, first + h))
    here = pl.BlockSpec((rows, HD), lambda h, *_: (0, h))
    return pl.pallas_call(
        functools.partial(forward_kernel, n_pool, blocks, list_len, heads),
        grid_spec=pltpu.PrefetchScalarGridSpec(
            num_scalar_prefetch=2,
            grid=(heads,),
            in_specs=[column, column] + [pl.BlockSpec(memory_space=pl.ANY)] * n_pool,
            out_specs=[
                here,
                pl.BlockSpec((1, rows, keys), lambda h, *_: (h, 0, 0)),
                pl.BlockSpec((rows, HD), lambda h, *_: (0, 0)),
            ],
            scratch_shapes=[
                pltpu.VMEM((2, n_pool, 2 * rows, HD), jnp.bfloat16),
                pltpu.SemaphoreType.DMA((2, n_pool)),
            ],
        ),
        out_shape=[
            jax.ShapeDtypeStruct((rows, heads * HD), jnp.float32),
            jax.ShapeDtypeStruct((heads, rows, keys), jnp.bfloat16),
            jax.ShapeDtypeStruct((rows, HD), jnp.float32),
        ],
        compiler_params=pltpu.CompilerParams(vmem_limit_bytes=VMEM),
        cost_estimate=pl.CostEstimate(
            flops=4 * heads * rows * keys * HD,
            bytes_accessed=heads * (n_pool * 4 * rows * HD + rows * keys * 2 + rows * HD * 8),
            transcendentals=heads * rows * keys,
        ),
        name="forward",
    )(where, counts, queries, ref, *pool)


def backward(where, queries, policy, ref, attn, probs, inv, pool, first, heads, blocks, list_len):
    rows, keys = blocks * BLK, list_len * BLK
    n_pool = len(pool)
    column = pl.BlockSpec((rows, HD), lambda h, *_: (0, first + h))
    here = pl.BlockSpec((rows, HD), lambda h, *_: (0, h))
    anywhere = pl.BlockSpec(memory_space=pl.ANY)
    return pl.pallas_call(
        functools.partial(backward_kernel, n_pool, blocks, list_len, heads),
        grid_spec=pltpu.PrefetchScalarGridSpec(
            num_scalar_prefetch=1,
            grid=(heads,),
            in_specs=[
                column,
                column,
                column,
                here,
                pl.BlockSpec((1, rows, keys), lambda h, *_: (h, 0, 0)),
                pl.BlockSpec((rows, HD), lambda h, *_: (0, 0)),
            ]
            + [anywhere] * n_pool,
            out_specs=[here] + [anywhere] * n_pool,
            scratch_shapes=[
                pltpu.VMEM((2, n_pool, 2 * rows, HD), jnp.bfloat16),
                pltpu.SemaphoreType.DMA((2, n_pool)),
                pltpu.VMEM((2, n_pool, 2 * rows, HD), jnp.bfloat16),
                pltpu.SemaphoreType.DMA((2, n_pool)),
            ],
        ),
        out_shape=[jax.ShapeDtypeStruct((rows, heads * HD), jnp.bfloat16)]
        + [jax.ShapeDtypeStruct((2 * rows, heads * HD), jnp.bfloat16)] * n_pool,
        compiler_params=pltpu.CompilerParams(vmem_limit_bytes=VMEM),
        cost_estimate=pl.CostEstimate(
            flops=8 * heads * rows * keys * HD,
            bytes_accessed=heads * (n_pool * 8 * rows * HD + rows * keys * 2 + rows * HD * 12),
            transcendentals=0,
        ),
        name="backward",
    )(where, queries, policy, ref, attn, probs, inv, *pool)


def shift(value, steps):
    count = lax.axis_size("frame")
    pairs = [(s, s + steps) for s in range(count) if 0 <= s + steps < count]
    return lax.ppermute(value, "frame", pairs)


def swap(value, bit):
    count = lax.axis_size("frame")
    return lax.ppermute(value, "frame", [(s, s ^ bit) for s in range(count)])


def add(*terms):
    total = terms[0].astype(jnp.float32)
    for term in terms[1:]:
        total = total + term.astype(jnp.float32)
    return total.astype(jnp.bfloat16)


def gather(kv, corner, upper, levels):
    far = [(shift(kv, 4), shift(kv, -4))]
    across, along = swap(kv, 1), swap(kv, 2)
    for level in range(3, levels):
        step = 1 << (level - 1)
        far.append((shift(far[-1][0], step), shift(far[-1][1], -step)))
    cross = swap(jnp.where(upper, far[0][0], far[0][1]), 2)
    diagonal = swap(jnp.where(corner, along, cross), 1)
    return [kv, across, along, cross, diagonal] + [x for pair in far for x in pair]


def scatter(parts, corner, upper, levels):
    own, across, along, cross, diagonal = parts[:5]
    before, after = list(parts[5::2]), list(parts[6::2])
    zero = jnp.zeros((), jnp.bfloat16)
    diagonal = swap(diagonal, 1)
    across = swap(across, 1)
    for level in range(levels - 1, 2, -1):
        step = 1 << (level - 1)
        n = level - 2
        back, forth = shift(before[n], -step), shift(after[n], step)
        if n > 1:
            before[n - 1], after[n - 1] = add(before[n - 1], back), add(after[n - 1], forth)
        else:
            extra = (back, forth)
    cross = swap(add(cross, jnp.where(corner, zero, diagonal)), 2)
    along = swap(add(along, jnp.where(corner, diagonal, zero)), 2)
    more = extra if levels > 3 else (zero, zero)
    first = add(before[0], more[0], jnp.where(upper, cross, zero))
    second = add(after[0], more[1], jnp.where(upper, zero, cross))
    return add(own, across, along, shift(first, -4), shift(second, 4))


def places(gap, me, levels):
    corner_of = me % 4
    upper = corner_of >= 2
    odd = corner_of % 2 == 1
    at = jnp.zeros_like(gap)
    before_1 = jnp.where(odd, 1, 4)
    after_1 = jnp.where(odd, 4, 1)
    before_2 = jnp.where(upper, 2, 3)
    after_2 = jnp.where(upper, 3, 2)
    at = at + jnp.where(gap == -1, before_1, 0) + jnp.where(gap == 1, after_1, 0)
    at = at + jnp.where(gap == -2, before_2, 0) + jnp.where(gap == 2, after_2, 0)
    for level in range(2, levels):
        at = at + jnp.where(gap == -(1 << level), 1 + 2 * level, 0)
        at = at + jnp.where(gap == (1 << level), 2 + 2 * level, 0)
    return at


def chunk_count(heads):
    for n in (4, 2):
        if heads % n == 0:
            return n
    return 1


def local(queries, keys, values, policy_grad, ref_velocity, key_lists, frame_tokens):
    rows, cols = queries.shape
    heads = cols // HD
    blocks = rows // BLK
    list_len = key_lists.shape[1]
    levels = lax.axis_size("frame").bit_length() - 1
    all_features = cols * lax.axis_size("head")
    me = lax.axis_index("frame")
    corner_of = me % 4
    corner = (corner_of == 0) | (corner_of == 3)
    upper = corner_of >= 2
    where = (places(key_lists // blocks - me, me, levels) * blocks + key_lists % blocks).reshape(-1)
    ids = jnp.arange(frame_tokens.shape[0], dtype=jnp.int32)
    counts = jnp.sum(
        jnp.where(key_lists.reshape(-1, 1) == ids[None, :], frame_tokens[None, :], 0), axis=-1
    ).astype(jnp.int32)
    n_chunks = chunk_count(heads)
    each = heads // n_chunks
    wide = each * HD
    pools, forwards = [], []
    for c in range(n_chunks):
        cut = slice(c * wide, (c + 1) * wide)
        kv = jnp.concatenate([keys[:, cut], values[:, cut]], axis=0)
        pools.append(gather(kv, corner, upper, levels))
    for c in range(n_chunks):
        forwards.append(
            forward(
                where, counts, queries, ref_velocity, pools[c], c * each, each, blocks, list_len
            )
        )
    squares = sum(f[2] for f in forwards)
    kl = lax.psum(jnp.sum(squares, axis=-1), "head") / all_features
    inv = jnp.broadcast_to((1.0 / (1.0 + kl))[:, None], (rows, HD))
    grad_q, grad_k, grad_v = [], [], []
    for c in range(n_chunks):
        attn, probs, _ = forwards[c]
        dq, *parts = backward(
            where, queries, policy_grad, ref_velocity, attn, probs, inv,
            pools[c], c * each, each, blocks, list_len,
        )
        total = scatter(parts, corner, upper, levels)
        grad_q.append(dq)
        grad_k.append(total[:rows])
        grad_v.append(total[rows:])
    return tuple(jnp.concatenate(x, axis=1) for x in (grad_q, grad_k, grad_v))


def solution(mesh):
    cut = P("frame", "head")
    return jax.shard_map(
        local,
        mesh=mesh,
        in_specs=(cut,) * 5 + (P("frame", None), P()),
        out_specs=(cut,) * 3,
        check_vma=False,
    )
```

time: 836 us -> 436 us (0.52)
  local copies, waits for them, and re-layouts: 252 us -> 33.6 us
  matrix products: 107 us -> 0 us
  waiting for transfers between devices: 240 us -> 165 us
  Pallas kernels: 0 us -> 73.7 us
  starting transfers between devices: 173 us -> 133 us
  other arithmetic: 51.9 us -> 22.1 us
    dot_general x8 -> x0, matrix products: 107 us -> none  [the longest x1 25.8 us: local(): jnp.dot(selector, part_k, precision=lax.Precision.HIGHEST)]
    reshape x6 -> x1, local copies, waits for them, and re-layouts: 82.2 us -> 0.08 us  [local(): (places(key_lists // blocks - me, me, levels) * blocks + key_lists % bloc...]
    ppermute x32 -> x64, waiting for transfers between devices: 240 us -> 165 us  [the longest x32 125 us: swap(): return lax.ppermute(value, 'frame', [(s, s ^ bit) for s in range(count)])]
    pallas_call x0 -> x8, Pallas kernels: none -> 73.7 us  [the longest x4 41.9 us: backward(): pl.pallas_call(functools.partial(backward_kernel, n_pool, blocks, list_le...]
    slice x2 -> x5, local copies, waits for them, and re-layouts: 50.3 us -> 2.16 us  [the longest x1 1.92 us: local(): kv = jnp.concatenate([keys[:, cut], values[:, cut]], axis=0)]
    ppermute x32 -> x64, starting transfers between devices: 173 us -> 133 us  [the longest x32 92.4 us: shift(): return lax.ppermute(value, 'frame', pairs)]
    mul x1 -> x0, local copies, waits for them, and re-layouts: 24.4 us -> none  [local(): jnp.einsum('bhqk,bqhd->bkhd', grad_scores16, query4, preferred_element_ty...]
    sub x1 -> x0, other arithmetic: 18.8 us -> none  [local(): expd = jnp.exp(scores - highest)]
  transfers between devices with their start and end apart: 32 -> 64, of which waited for: 12 -> 33; matrix products, arithmetic and copies ran while one was open for 24% -> 4% of each run, Pallas kernels for 0% -> 13%
where the time goes in v1:
time: 436 us; the launch traced here: 432 us
  waiting for transfers between devices  165 us (38%)
  starting transfers between devices  133 us (31%)
  Pallas kernels  73.7 us (17%)
  local copies, waits for them, and re-layouts  33.6 us (8%)
  other arithmetic  22.1 us (5%)
    ppermute x32, waiting for transfers between devices, swap(): return lax.ppermute(value, 'frame', [(s, s ^ bit) for s in range(count)])  125 us
    ppermute x32, starting transfers between devices, shift(): return lax.ppermute(value, 'frame', pairs)  92.4 us
    pallas_call x4, Pallas kernels, backward(): pl.pallas_call(functools.partial(backward_kernel, n_pool, blocks, list_le...  41.9 us
    ppermute x32, waiting for transfers between devices, shift(): return lax.ppermute(value, 'frame', pairs)  40.8 us
    ppermute x32, starting transfers between devices, swap(): return lax.ppermute(value, 'frame', [(s, s ^ bit) for s in range(count)])  40.2 us
    pallas_call x4, Pallas kernels, forward(): pl.pallas_call(functools.partial(forward_kernel, n_pool, blocks, list_len...  31.7 us
    unnamed x184, local copies, waits for them, and re-layouts  31.2 us
    convert_element_type x12, other arithmetic, add(): return total.astype(jnp.bfloat16)  10.1 us
  transfers between devices with their start and end apart: 64, of which 33 were waited for; matrix products, arithmetic and copies ran while one was open for 4% of the time, Pallas kernels for 13%

profile of v1, /device:TPU:16, one launch (start us, length us, event | category | flops | bytes accessed | tf_op | source)
XLA Modules:
  0.0 431.7 jit_solution(10218409995336393533)
XLA Ops:
  0.6 1.9 fusion.9
  3.5 2.3 collective-permute-start.19
  5.8 4.3 collective-permute-start.18
  14.5 4.0 collective-permute-start.26
  18.6 4.7 %collective-permute-done.19.rest_6_ = bf16[512,640]{1,0:T(8,128)(2,1)} collective-permute-done((bf16[512,640]{1,0:T(8,128)(2,1)}, bf16[512,640]{1,0:T(8,128)(2,1)}, u32[]{:S(2)}, u32[]{:S(2)}) %collective-permute-start.19) | collective-permute-done | bytes 655392 | tf_op jit(solution)/shard_map/ppermute | solution.py:236
  25.7 1.9 collective-permute-start.3
  28.1 3.5 collective-permute-start.2
  31.7 5.6 %collective-permute-done.27.rest_6_ = bf16[512,640]{1,0:T(8,128)(2,1)S(1)} collective-permute-done((bf16[512,640]{1,0:T(8,128)(2,1)}, bf16[512,640]{1,0:T(8,128)(2,1)S(1)}, u32[]{:S(2)}, u32[]{:S(2)}) %collective-permute-start.27) | collective-permute-done | bytes 655392 | tf_op jit(solution)/shard_map/ppermute | solution.py:236
  41.3 2.3 collective-permute-start.11
  43.6 7.7 %collective-permute-done.3.rest_6_ = bf16[512,640]{1,0:T(8,128)(2,1)S(1)} collective-permute-done((bf16[512,640]{1,0:T(8,128)(2,1)S(1)}, bf16[512,640]{1,0:T(8,128)(2,1)S(1)}, u32[]{:S(2)}, u32[]{:S(2)}) %collective-permute-start.3) | collective-permute-done | bytes 655392 | tf_op jit(solution)/shard_map/ppermute | solution.py:236
  51.3 1.9 collective-permute-start.10
  56.1 2.7 collective-permute-start.9
  59.3 4.9 %collective-permute-done.11.rest_6_ = bf16[512,640]{1,0:T(8,128)(2,1)} collective-permute-done((bf16[512,640]{1,0:T(8,128)(2,1)S(1)}, bf16[512,640]{1,0:T(8,128)(2,1)}, u32[]{:S(2)}, u32[]{:S(2)}) %collective-permute-start.11) | collective-permute-done | bytes 655392 | tf_op jit(solution)/shard_map/ppermute | solution.py:236
  65.8 2.0 collective-permute-done.10.rest_5_
  69.3 2.0 broadcast_select_fusion.6
  74.6 3.9 collective-permute-start.31
  78.5 4.5 %collective-permute-done.8.rest_1_ = bf16[512,640]{1,0:T(8,128)(2,1)S(1)} collective-permute-done((bf16[512,640]{1,0:T(8,128)(2,1)S(1)}, bf16[512,640]{1,0:T(8,128)(2,1)S(1)}, u32[]{:S(2)}, u32[]{:S(2)}) %collective-permute-start.8) | collective-permute-done | bytes 655392 | tf_op jit(solution)/shard_map/ppermute | solution.py:241
  85.4 3.0 collective-permute-done.20.rest_3_
  88.4 2.7 collective-permute-start.30
  91.2 11.4 %collective-permute-done.4.rest_3_ = bf16[512,640]{1,0:T(8,128)(2,1)} collective-permute-done((bf16[512,640]{1,0:T(8,128)(2,1)S(1)}, bf16[512,640]{1,0:T(8,128)(2,1)}, u32[]{:S(2)}, u32[]{:S(2)}) %collective-permute-start.4) | collective-permute-done | bytes 655392 | tf_op jit(solution)/shard_map/ppermute | solution.py:241
  102.6 4.1 collective-permute-start.7
  106.8 9.8 %collective-permute-done.12.rest_3_ = bf16[512,640]{1,0:T(8,128)(2,1)} collective-permute-done((bf16[512,640]{1,0:T(8,128)(2,1)}, bf16[512,640]{1,0:T(8,128)(2,1)}, u32[]{:S(2)}, u32[]{:S(2)}) %collective-permute-start.12) | collective-permute-done | bytes 655392 | tf_op jit(solution)/shard_map/ppermute | solution.py:241
  116.6 2.7 collective-permute-start.6
  119.5 3.2 collective-permute-start.15
  122.7 4.8 %collective-permute-done.28.rest_3_ = bf16[512,640]{1,0:T(8,128)(2,1)} collective-permute-done((bf16[512,640]{1,0:T(8,128)(2,1)}, bf16[512,640]{1,0:T(8,128)(2,1)}, u32[]{:S(2)}, u32[]{:S(2)}) %collective-permute-start.28) | collective-permute-done | bytes 655392 | tf_op jit(solution)/shard_map/ppermute | solution.py:241
  127.6 2.9 collective-permute-start.14
  137.5 5.9 %collective-permute-done.14.rest_7_ = bf16[512,640]{1,0:T(8,128)(2,1)S(1)} collective-permute-done((bf16[512,640]{1,0:T(8,128)(2,1)}, bf16[512,640]{1,0:T(8,128)(2,1)S(1)}, u32[]{:S(2)}, u32[]{:S(2)}) %collective-permute-start.14) | collective-permute-done | bytes 655392 | tf_op jit(solution)/shard_map/ppermute | solution.py:236
  144.2 3.9 collective-permute-start.23
  149.0 2.7 collective-permute-start.22
  151.8 10.4 %collective-permute-done.13.rest_4_ = bf16[512,640]{1,0:T(8,128)(2,1)S(1)} collective-permute-done((bf16[512,640]{1,0:T(8,128)(2,1)S(1)}, bf16[512,640]{1,0:T(8,128)(2,1)S(1)}, u32[]{:S(2)}, u32[]{:S(2)}) %collective-permute-start.13) | collective-permute-done | bytes 655392 | tf_op jit(solution)/shard_map/ppermute | solution.py:241
  170.6 8.1 %forward.5 = (f32[256,640]{1,0:T(8,128)S(1)}, bf16[5,256,768]{2,1,0:T(8,128)(2,1)S(1)}, f32[256,128]{1,0:T(8,128)S(1)}) custom-call(s32[12]{0:T(128)S(1)} %reshape.13.where_ref, s32[12]{0:T(128)S(1)} %select_reduce_fusion.count_ref, bf16[256,2560]{1,0:T(8,128)(2,1)S(1)} %copy-done, bf16[256,2560]{1,0:T(8,128)(2,1)S(1)} %copy-done.1, ...), custom_call_target="tpu_custom_call" | custom-call | flops 503316480 | bytes 9175040 | tf_op jit(solution)/shard_map/forward/pallas_call | solution.py:162
  180.0 7.9 %forward.4 = (f32[256,640]{1,0:T(8,128)S(1)}, bf16[5,256,768]{2,1,0:T(8,128)(2,1)S(1)}, f32[256,128]{1,0:T(8,128)S(1)}) custom-call(s32[12]{0:T(128)S(1)} %reshape.13.where_ref, s32[12]{0:T(128)S(1)} %select_reduce_fusion.count_ref, bf16[256,2560]{1,0:T(8,128)(2,1)S(1)} %copy-done, bf16[256,2560]{1,0:T(8,128)(2,1)S(1)} %copy-done.1, ...), custom_call_target="tpu_custom_call" | custom-call | flops 503316480 | bytes 9175040 | tf_op jit(solution)/shard_map/forward/pallas_call | solution.py:162
  189.3 7.9 %forward.7 = (f32[256,640]{1,0:T(8,128)S(1)}, bf16[5,256,768]{2,1,0:T(8,128)(2,1)S(1)}, f32[256,128]{1,0:T(8,128)S(1)}) custom-call(s32[12]{0:T(128)S(1)} %reshape.13.where_ref, s32[12]{0:T(128)S(1)} %select_reduce_fusion.count_ref, bf16[256,2560]{1,0:T(8,128)(2,1)S(1)} %copy-done, bf16[256,2560]{1,0:T(8,128)(2,1)S(1)} %copy-done.1, ...), custom_call_target="tpu_custom_call" | custom-call | flops 503316480 | bytes 9175040 | tf_op jit(solution)/shard_map/forward/pallas_call | solution.py:162
  200.3 7.9 %forward.6 = (f32[256,640]{1,0:T(8,128)S(1)}, bf16[5,256,768]{2,1,0:T(8,128)(2,1)S(1)}, f32[256,128]{1,0:T(8,128)S(1)}) custom-call(s32[12]{0:T(128)S(1)} %reshape.13.where_ref, s32[12]{0:T(128)S(1)} %select_reduce_fusion.count_ref, bf16[256,2560]{1,0:T(8,128)(2,1)S(1)} %copy-done, bf16[256,2560]{1,0:T(8,128)(2,1)S(1)} %copy-done.1, ...), custom_call_target="tpu_custom_call" | custom-call | flops 503316480 | bytes 9175040 | tf_op jit(solution)/shard_map/forward/pallas_call | solution.py:162
  210.5 2.5 psum.7
  216.3 10.2 %backward.7 = (bf16[256,640]{1,0:T(8,128)(2,1)S(1)}, bf16[512,640]{1,0:T(8,128)(2,1)S(1)}, bf16[512,640]{1,0:T(8,128)(2,1)}, bf16[512,640]{1,0:T(8,128)(2,1)S(1)...) custom-call(s32[12]{0:T(128)S(1)} %reshape.13.where_ref, ...), custom_call_target="tpu_custom_call" | custom-call | flops 1006632960 | bytes 15728640 | tf_op jit(solution)/shard_map/backward/pallas_call | solution.py:199
  229.4 2.8 collective-permute-start.59
  232.3 4.0 collective-permute-start.62
  236.4 10.6 %backward.6 = (bf16[256,640]{1,0:T(8,128)(2,1)S(1)}, bf16[512,640]{1,0:T(8,128)(2,1)S(1)}, bf16[512,640]{1,0:T(8,128)(2,1)}, bf16[512,640]{1,0:T(8,128)(2,1)S(1)...) custom-call(s32[12]{0:T(128)S(1)} %reshape.13.where_ref, ...), custom_call_target="tpu_custom_call" | custom-call | flops 1006632960 | bytes 15728640 | tf_op jit(solution)/shard_map/backward/pallas_call | solution.py:199
  252.6 10.4 %backward.5 = (bf16[256,640]{1,0:T(8,128)(2,1)S(1)}, bf16[512,640]{1,0:T(8,128)(2,1)S(1)}, bf16[512,640]{1,0:T(8,128)(2,1)S(1)}, bf16[512,640]{1,0:T(8,128)(2,1)...) custom-call(s32[12]{0:T(128)S(1)} %reshape.13.where_ref, ...), custom_call_target="tpu_custom_call" | custom-call | flops 1006632960 | bytes 15728640 | tf_op jit(solution)/shard_map/backward/pallas_call | solution.py:199
  268.1 10.7 %backward.4 = (bf16[256,640]{1,0:T(8,128)(2,1)S(1)}, bf16[512,640]{1,0:T(8,128)(2,1)S(1)}, bf16[512,640]{1,0:T(8,128)(2,1)S(1)}, bf16[512,640]{1,0:T(8,128)(2,1)...) custom-call(s32[12]{0:T(128)S(1)} %reshape.13.where_ref, ...), custom_call_target="tpu_custom_call" | custom-call | flops 1006632960 | bytes 15728640 | tf_op jit(solution)/shard_map/backward/pallas_call | solution.py:199
  280.4 2.0 collective-permute-start.51
  287.3 3.9 collective-permute-start.54
  291.1 5.4 %collective-permute-done.49 = bf16[512,640]{1,0:T(8,128)(2,1)S(1)} collective-permute-done((bf16[512,640]{1,0:T(8,128)(2,1)S(1)}, bf16[512,640]{1,0:T(8,128)(2,1)S(1)}, u32[]{:S(2)}, u32[]{:S(2)}) %collective-permute-start.49) | collective-permute-done | bytes 655392 | tf_op jit(solution)/shard_map/ppermute | solution.py:241
  296.5 2.0 collective-permute-start.43
  300.4 10.1 %collective-permute-done.41 = bf16[512,640]{1,0:T(8,128)(2,1)S(1)} collective-permute-done((bf16[512,640]{1,0:T(8,128)(2,1)S(1)}, bf16[512,640]{1,0:T(8,128)(2,1)S(1)}, u32[]{:S(2)}, u32[]{:S(2)}) %collective-permute-start.41) | collective-permute-done | bytes 655392 | tf_op jit(solution)/shard_map/ppermute | solution.py:241
  310.6 1.9 collective-permute-start.46
  312.5 9.9 %collective-permute-done.33 = bf16[512,640]{1,0:T(8,128)(2,1)S(1)} collective-permute-done((bf16[512,640]{1,0:T(8,128)(2,1)}, bf16[512,640]{1,0:T(8,128)(2,1)S(1)}, u32[]{:S(2)}, u32[]{:S(2)}) %collective-permute-start.33) | collective-permute-done | bytes 655392 | tf_op jit(solution)/shard_map/ppermute | solution.py:241
  324.6 2.0 collective-permute-start.35
  326.6 3.9 collective-permute-start.38
  334.5 5.5 %collective-permute-done.52 = bf16[512,640]{1,0:T(8,128)(2,1)S(1)} collective-permute-done((bf16[512,640]{1,0:T(8,128)(2,1)S(1)}, bf16[512,640]{1,0:T(8,128)(2,1)S(1)}, u32[]{:S(2)}, u32[]{:S(2)}) %collective-permute-start.52) | collective-permute-done | bytes 655392 | tf_op jit(solution)/shard_map/ppermute | solution.py:241
  342.8 3.6 collective-permute-start.61
  346.5 7.6 %collective-permute-done.44 = bf16[512,640]{1,0:T(8,128)(2,1)S(1)} collective-permute-done((bf16[512,640]{1,0:T(8,128)(2,1)S(1)}, bf16[512,640]{1,0:T(8,128)(2,1)S(1)}, u32[]{:S(2)}, u32[]{:S(2)}) %collective-permute-start.44) | collective-permute-done | bytes 655392 | tf_op jit(solution)/shard_map/ppermute | solution.py:241
  356.6 11.6 %collective-permute-done.58 = bf16[512,640]{1,0:T(8,128)(2,1)S(1)} collective-permute-done((bf16[512,640]{1,0:T(8,128)(2,1)S(1)}, bf16[512,640]{1,0:T(8,128)(2,1)S(1)}, u32[]{:S(2)}, u32[]{:S(2)}) %collective-permute-start.58) | collective-permute-done | bytes 655392 | tf_op jit(solution)/shard_map/ppermute | solution.py:241
  368.1 2.0 collective-permute-start.53
  370.1 12.0 %collective-permute-done.36 = bf16[512,640]{1,0:T(8,128)(2,1)S(1)} collective-permute-done((bf16[512,640]{1,0:T(8,128)(2,1)S(1)}, bf16[512,640]{1,0:T(8,128)(2,1)S(1)}, u32[]{:S(2)}, u32[]{:S(2)}) %collective-permute-start.36) | collective-permute-done | bytes 655392 | tf_op jit(solution)/shard_map/ppermute | solution.py:241
  384.7 8.4 %collective-permute-done.50 = bf16[512,640]{1,0:T(8,128)(2,1)S(1)} collective-permute-done((bf16[512,640]{1,0:T(8,128)(2,1)S(1)}, bf16[512,640]{1,0:T(8,128)(2,1)S(1)}, u32[]{:S(2)}, u32[]{:S(2)}) %collective-permute-start.50) | collective-permute-done | bytes 655392 | tf_op jit(solution)/shard_map/ppermute | solution.py:241
  396.1 2.2 collective-permute-start.45
  399.8 4.1 collective-permute-start.47
  406.0 4.7 %collective-permute-done.40 = bf16[512,640]{1,0:T(8,128)(2,1)S(1)} collective-permute-done((bf16[512,640]{1,0:T(8,128)(2,1)S(1)}, bf16[512,640]{1,0:T(8,128)(2,1)S(1)}, u32[]{:S(2)}, u32[]{:S(2)}) %collective-permute-start.40) | collective-permute-done | bytes 655392 | tf_op jit(solution)/shard_map/ppermute | solution.py:241
  412.2 2.0 collective-permute-start.37
  414.2 3.9 collective-permute-start.39
  421.8 3.1 collective-permute-done.37
  424.9 4.0 collective-permute-done.39
  (296 shorter events, 103.4 us)
Async XLA Ops:
  3.5 19.8 %collective-permute-start.19 = (bf16[512,640]{1,0:T(8,128)(2,1)}, bf16[512,640]{1,0:T(8,128)(2,1)}, u32[]{:S(2)}, u32[]{:S(2)}) collective-permute-start(bf16[512,640]{1,0:T(8,128)(2,1)} %pad_maximum_fusion.5.rest_0_), channel_id=1, source_target_pairs={{8,0},{10,2},{12,4},{14,6},{16,8},{18,10},{20,12},{22,14},{24,16},... | collective-permute-start | bytes 1966088 | tf_op jit(solution)/shard_map/ppermute | solution.py:236
  5.8 19.9 %collective-permute-start.18 = (bf16[512,640]{1,0:T(8,128)(2,1)}, bf16[512,640]{1,0:T(8,128)(2,1)}, u32[]{:S(2)}, u32[]{:S(2)}) collective-permute-start(bf16[512,640]{1,0:T(8,128)(2,1)} %pad_maximum_fusion.5.rest_0_), channel_id=1, source_target_pairs={{0,8},{2,10},{4,12},{6,14},{8,16},{10,18},{12,20},{14,22},{16,24},... | collective-permute-start | bytes 1966088 | tf_op jit(solution)/shard_map/ppermute | solution.py:236
  10.1 17.9 %collective-permute-start.17 = (bf16[512,640]{1,0:T(8,128)(2,1)}, bf16[512,640]{1,0:T(8,128)(2,1)S(1)}, u32[]{:S(2)}, u32[]{:S(2)}) collective-permute-start(bf16[512,640]{1,0:T(8,128)(2,1)} %pad_maximum_fusion.5.rest_0_), channel_id=1, source_target_pairs={{0,4},{2,6},{4,0},{6,2},{8,12},{10,14},{12,8},{14,10},{16,20},{18,... | collective-permute-start | bytes 1966088 | tf_op jit(solution)/shard_map/ppermute | solution.py:241
  12.6 24.6 %collective-permute-start.27 = (bf16[512,640]{1,0:T(8,128)(2,1)}, bf16[512,640]{1,0:T(8,128)(2,1)S(1)}, u32[]{:S(2)}, u32[]{:S(2)}) collective-permute-start(bf16[512,640]{1,0:T(8,128)(2,1)} %pad_maximum_fusion.6.rest_0_), channel_id=1, source_target_pairs={{8,0},{10,2},{12,4},{14,6},{16,8},{18,10},{20,12},{22,14},{24,16},... | collective-permute-start | bytes 1966088 | tf_op jit(solution)/shard_map/ppermute | solution.py:236
  14.5 25.2 %collective-permute-start.26 = (bf16[512,640]{1,0:T(8,128)(2,1)}, bf16[512,640]{1,0:T(8,128)(2,1)}, u32[]{:S(2)}, u32[]{:S(2)}) collective-permute-start(bf16[512,640]{1,0:T(8,128)(2,1)} %pad_maximum_fusion.6.rest_0_), channel_id=1, source_target_pairs={{0,8},{2,10},{4,12},{6,14},{8,16},{10,18},{12,20},{14,22},{16,24},... | collective-permute-start | bytes 1966088 | tf_op jit(solution)/shard_map/ppermute | solution.py:236
  23.3 18.0 %collective-permute-start.25 = (bf16[512,640]{1,0:T(8,128)(2,1)}, bf16[512,640]{1,0:T(8,128)(2,1)S(1)}, u32[]{:S(2)}, u32[]{:S(2)}) collective-permute-start(bf16[512,640]{1,0:T(8,128)(2,1)} %pad_maximum_fusion.6.rest_0_), channel_id=1, source_target_pairs={{0,4},{2,6},{4,0},{6,2},{8,12},{10,14},{12,8},{14,10},{16,20},{18,... | collective-permute-start | bytes 1966088 | tf_op jit(solution)/shard_map/ppermute | solution.py:241
  25.7 25.6 %collective-permute-start.3 = (bf16[512,640]{1,0:T(8,128)(2,1)S(1)}, bf16[512,640]{1,0:T(8,128)(2,1)S(1)}, u32[]{:S(2)}, u32[]{:S(2)}) collective-permute-start(bf16[512,640]{1,0:T(8,128)(2,1)S(1)} %pad_maximum_fusion.3.rest_0_), channel_id=1, source_target_pairs={{8,0},{10,2},{12,4},{14,6},{16,8},{18,10},{20,12},{22,14},{24,16},... | collective-permute-start | bytes 1966088 | tf_op jit(solution)/shard_map/ppermute | solution.py:236
  28.1 26.3 %collective-permute-start.2 = (bf16[512,640]{1,0:T(8,128)(2,1)S(1)}, bf16[512,640]{1,0:T(8,128)(2,1)}, u32[]{:S(2)}, u32[]{:S(2)}) collective-permute-start(bf16[512,640]{1,0:T(8,128)(2,1)S(1)} %pad_maximum_fusion.3.rest_0_), channel_id=1, source_target_pairs={{0,8},{2,10},{4,12},{6,14},{8,16},{10,18},{12,20},{14,22},{16,24},... | collective-permute-start | bytes 1966088 | tf_op jit(solution)/shard_map/ppermute | solution.py:236
  37.2 18.8 %collective-permute-start.24 = (bf16[512,640]{1,0:T(8,128)(2,1)}, bf16[512,640]{1,0:T(8,128)(2,1)}, u32[]{:S(2)}, u32[]{:S(2)}) collective-permute-start(bf16[512,640]{1,0:T(8,128)(2,1)} %pad_maximum_fusion.6.rest_0_), channel_id=1, source_target_pairs={{0,2},{2,0},{4,6},{6,4},{8,10},{10,8},{12,14},{14,12},{16,18},{18,... | collective-permute-start | bytes 1966088 | tf_op jit(solution)/shard_map/ppermute | solution.py:241
  39.7 19.0 %collective-permute-start.1 = (bf16[512,640]{1,0:T(8,128)(2,1)S(1)}, bf16[512,640]{1,0:T(8,128)(2,1)S(1)}, u32[]{:S(2)}, u32[]{:S(2)}) collective-permute-start(bf16[512,640]{1,0:T(8,128)(2,1)S(1)} %pad_maximum_fusion.3.rest_0_), channel_id=1, source_target_pairs={{0,4},{2,6},{4,0},{6,2},{8,12},{10,14},{12,8},{14,10},{16,20},{18,... | collective-permute-start | bytes 1966088 | tf_op jit(solution)/shard_map/ppermute | solution.py:241
  41.3 23.0 %collective-permute-start.11 = (bf16[512,640]{1,0:T(8,128)(2,1)S(1)}, bf16[512,640]{1,0:T(8,128)(2,1)}, u32[]{:S(2)}, u32[]{:S(2)}) collective-permute-start(bf16[512,640]{1,0:T(8,128)(2,1)S(1)} %pad_maximum_fusion.4.rest_0_), channel_id=1, source_target_pairs={{8,0},{10,2},{12,4},{14,6},{16,8},{18,10},{20,12},{22,14},{24,16},... | collective-permute-start | bytes 1966088 | tf_op jit(solution)/shard_map/ppermute | solution.py:236
  51.3 16.5 %collective-permute-start.10 = (bf16[512,640]{1,0:T(8,128)(2,1)S(1)}, bf16[512,640]{1,0:T(8,128)(2,1)}, u32[]{:S(2)}, u32[]{:S(2)}) collective-permute-start(bf16[512,640]{1,0:T(8,128)(2,1)S(1)} %pad_maximum_fusion.4.rest_0_), channel_id=1, source_target_pairs={{0,8},{2,10},{4,12},{6,14},{8,16},{10,18},{12,20},{14,22},{16,24},... | collective-permute-start | bytes 1966088 | tf_op jit(solution)/shard_map/ppermute | solution.py:236
  54.4 17.7 %collective-permute-start = (bf16[512,640]{1,0:T(8,128)(2,1)S(1)}, bf16[512,640]{1,0:T(8,128)(2,1)S(1)}, u32[]{:S(2)}, u32[]{:S(2)}) collective-permute-start(bf16[512,640]{1,0:T(8,128)(2,1)S(1)} %pad_maximum_fusion.3.rest_0_), channel_id=1, source_target_pairs={{0,2},{2,0},{4,6},{6,4},{8,10},{10,8},{12,14},{14,12},{16,18},{18,... | collective-permute-start | bytes 1966088 | tf_op jit(solution)/shard_map/ppermute | solution.py:241
  56.1 18.6 %collective-permute-start.9 = (bf16[512,640]{1,0:T(8,128)(2,1)S(1)}, bf16[512,640]{1,0:T(8,128)(2,1)S(1)}, u32[]{:S(2)}, u32[]{:S(2)}) collective-permute-start(bf16[512,640]{1,0:T(8,128)(2,1)S(1)} %pad_maximum_fusion.4.rest_0_), channel_id=1, source_target_pairs={{0,4},{2,6},{4,0},{6,2},{8,12},{10,14},{12,8},{14,10},{16,20},{18,... | collective-permute-start | bytes 1966088 | tf_op jit(solution)/shard_map/ppermute | solution.py:241
  58.7 24.3 %collective-permute-start.8 = (bf16[512,640]{1,0:T(8,128)(2,1)S(1)}, bf16[512,640]{1,0:T(8,128)(2,1)S(1)}, u32[]{:S(2)}, u32[]{:S(2)}) collective-permute-start(bf16[512,640]{1,0:T(8,128)(2,1)S(1)} %pad_maximum_fusion.4.rest_0_), channel_id=1, source_target_pairs={{0,2},{2,0},{4,6},{6,4},{8,10},{10,8},{12,14},{14,12},{16,18},{18,... | collective-permute-start | bytes 1966088 | tf_op jit(solution)/shard_map/ppermute | solution.py:241
  64.3 24.2 %collective-permute-start.20 = (bf16[512,640]{1,0:T(8,128)(2,1)S(1)}, bf16[512,640]{1,0:T(8,128)(2,1)S(1)}, u32[]{:S(2)}, u32[]{:S(2)}) collective-permute-start(bf16[512,640]{1,0:T(8,128)(2,1)S(1)} %broadcast_select_fusion.5), channel_id=1, source_target_pairs={{0,4},{2,6},{4,0},{6,2},{8,12},{10,14},{12,8},{14,10},{16,20},{18,... | collective-permute-start | bytes 1966088 | tf_op jit(solution)/shard_map/ppermute | solution.py:241
  67.8 34.7 %collective-permute-start.4 = (bf16[512,640]{1,0:T(8,128)(2,1)S(1)}, bf16[512,640]{1,0:T(8,128)(2,1)}, u32[]{:S(2)}, u32[]{:S(2)}) collective-permute-start(bf16[512,640]{1,0:T(8,128)(2,1)S(1)} %broadcast_select_fusion.7), channel_id=1, source_target_pairs={{0,4},{2,6},{4,0},{6,2},{8,12},{10,14},{12,8},{14,10},{16,20},{18,... | collective-permute-start | bytes 1966088 | tf_op jit(solution)/shard_map/ppermute | solution.py:241
  72.1 44.5 %collective-permute-start.12 = (bf16[512,640]{1,0:T(8,128)(2,1)}, bf16[512,640]{1,0:T(8,128)(2,1)}, u32[]{:S(2)}, u32[]{:S(2)}) collective-permute-start(bf16[512,640]{1,0:T(8,128)(2,1)} %broadcast_select_fusion.6), channel_id=1, source_target_pairs={{0,4},{2,6},{4,0},{6,2},{8,12},{10,14},{12,8},{14,10},{16,20},{18,... | collective-permute-start | bytes 1966088 | tf_op jit(solution)/shard_map/ppermute | solution.py:241
  74.6 44.9 %collective-permute-start.31 = (bf16[512,640]{1,0:T(8,128)(2,1)S(1)}, bf16[512,640]{1,0:T(8,128)(2,1)}, u32[]{:S(2)}, u32[]{:S(2)}) collective-permute-start(bf16[512,640]{1,0:T(8,128)(2,1)S(1)} %copy-done.16), channel_id=1, source_target_pairs={{8,0},{10,2},{12,4},{14,6},{16,8},{18,10},{20,12},{22,14},{24,16},... | collective-permute-start | bytes 1966088 | tf_op jit(solution)/shard_map/ppermute | solution.py:236
  83.9 43.6 %collective-permute-start.28 = (bf16[512,640]{1,0:T(8,128)(2,1)}, bf16[512,640]{1,0:T(8,128)(2,1)}, u32[]{:S(2)}, u32[]{:S(2)}) collective-permute-start(bf16[512,640]{1,0:T(8,128)(2,1)} %broadcast_select_fusion.4), channel_id=1, source_target_pairs={{0,4},{2,6},{4,0},{6,2},{8,12},{10,14},{12,8},{14,10},{16,20},{18,... | collective-permute-start | bytes 1966088 | tf_op jit(solution)/shard_map/ppermute | solution.py:241
  88.4 42.0 %collective-permute-start.30 = (bf16[512,640]{1,0:T(8,128)(2,1)}, bf16[512,640]{1,0:T(8,128)(2,1)}, u32[]{:S(2)}, u32[]{:S(2)}) collective-permute-start(bf16[512,640]{1,0:T(8,128)(2,1)} %collective-permute-done.26.rest_5_), channel_id=1, source_target_pairs={{0,8},{2,10},{4,12},{6,14},{8,16},{10,18},{12,20},{14,22},{16,24},... | collective-permute-start | bytes 1966088 | tf_op jit(solution)/shard_map/ppermute | solution.py:236
  102.6 28.4 %collective-permute-start.7 = (bf16[512,640]{1,0:T(8,128)(2,1)S(1)}, bf16[512,640]{1,0:T(8,128)(2,1)}, u32[]{:S(2)}, u32[]{:S(2)}) collective-permute-start(bf16[512,640]{1,0:T(8,128)(2,1)S(1)} %collective-permute-done.3.rest_6_), channel_id=1, source_target_pairs={{8,0},{10,2},{12,4},{14,6},{16,8},{18,10},{20,12},{22,14},{24,16},... | collective-permute-start | bytes 1966088 | tf_op jit(solution)/shard_map/ppermute | solution.py:236
  116.6 16.9 %collective-permute-start.6 = (bf16[512,640]{1,0:T(8,128)(2,1)}, bf16[512,640]{1,0:T(8,128)(2,1)S(1)}, u32[]{:S(2)}, u32[]{:S(2)}) collective-permute-start(bf16[512,640]{1,0:T(8,128)(2,1)} %collective-permute-done.2.rest_5_), channel_id=1, source_target_pairs={{0,8},{2,10},{4,12},{6,14},{8,16},{10,18},{12,20},{14,22},{16,24},... | collective-permute-start | bytes 1966088 | tf_op jit(solution)/shard_map/ppermute | solution.py:236
  119.5 16.8 %collective-permute-start.15 = (bf16[512,640]{1,0:T(8,128)(2,1)}, bf16[512,640]{1,0:T(8,128)(2,1)S(1)}, u32[]{:S(2)}, u32[]{:S(2)}) collective-permute-start(bf16[512,640]{1,0:T(8,128)(2,1)} %collective-permute-done.11.rest_6_), channel_id=1, source_target_pairs={{8,0},{10,2},{12,4},{14,6},{16,8},{18,10},{20,12},{22,14},{24,16},... | collective-permute-start | bytes 1966088 | tf_op jit(solution)/shard_map/ppermute | solution.py:236
  127.6 15.8 %collective-permute-start.14 = (bf16[512,640]{1,0:T(8,128)(2,1)}, bf16[512,640]{1,0:T(8,128)(2,1)S(1)}, u32[]{:S(2)}, u32[]{:S(2)}) collective-permute-start(bf16[512,640]{1,0:T(8,128)(2,1)} %collective-permute-done.10.rest_5_), channel_id=1, source_target_pairs={{0,8},{2,10},{4,12},{6,14},{8,16},{10,18},{12,20},{14,22},{16,24},... | collective-permute-start | bytes 1966088 | tf_op jit(solution)/shard_map/ppermute | solution.py:236
  130.4 17.7 %collective-permute-start.5 = (bf16[512,640]{1,0:T(8,128)(2,1)S(1)}, bf16[512,640]{1,0:T(8,128)(2,1)S(1)}, u32[]{:S(2)}, u32[]{:S(2)}) collective-permute-start(bf16[512,640]{1,0:T(8,128)(2,1)S(1)} %broadcast_select_fusion.3), channel_id=1, source_target_pairs={{0,2},{2,0},{4,6},{6,4},{8,10},{10,8},{12,14},{14,12},{16,18},{18,... | collective-permute-start | bytes 1966088 | tf_op jit(solution)/shard_map/ppermute | solution.py:241
  131.0 31.2 %collective-permute-start.13 = (bf16[512,640]{1,0:T(8,128)(2,1)S(1)}, bf16[512,640]{1,0:T(8,128)(2,1)S(1)}, u32[]{:S(2)}, u32[]{:S(2)}) collective-permute-start(bf16[512,640]{1,0:T(8,128)(2,1)S(1)} %broadcast_select_fusion.2), channel_id=1, source_target_pairs={{0,2},{2,0},{4,6},{6,4},{8,10},{10,8},{12,14},{14,12},{16,18},{18,... | collective-permute-start | bytes 1966088 | tf_op jit(solution)/shard_map/ppermute | solution.py:241
  133.5 55.7 %collective-permute-start.29 = (bf16[512,640]{1,0:T(8,128)(2,1)}, bf16[512,640]{1,0:T(8,128)(2,1)}, u32[]{:S(2)}, u32[]{:S(2)}) collective-permute-start(bf16[512,640]{1,0:T(8,128)(2,1)} %broadcast_select_fusion), channel_id=1, source_target_pairs={{0,2},{2,0},{4,6},{6,4},{8,10},{10,8},{12,14},{14,12},{16,18},{18,... | collective-permute-start | bytes 1966088 | tf_op jit(solution)/shard_map/ppermute | solution.py:241
  137.2 61.3 %collective-permute-start.16 = (bf16[512,640]{1,0:T(8,128)(2,1)}, bf16[512,640]{1,0:T(8,128)(2,1)}, u32[]{:S(2)}, u32[]{:S(2)}) collective-permute-start(bf16[512,640]{1,0:T(8,128)(2,1)} %pad_maximum_fusion.5.rest_0_), channel_id=1, source_target_pairs={{0,2},{2,0},{4,6},{6,4},{8,10},{10,8},{12,14},{14,12},{16,18},{18,... | collective-permute-start | bytes 1966088 | tf_op jit(solution)/shard_map/ppermute | solution.py:241
  144.2 54.3 %collective-permute-start.23 = (bf16[512,640]{1,0:T(8,128)(2,1)}, bf16[512,640]{1,0:T(8,128)(2,1)}, u32[]{:S(2)}, u32[]{:S(2)}) collective-permute-start(bf16[512,640]{1,0:T(8,128)(2,1)} %collective-permute-done.19.rest_6_), channel_id=1, source_target_pairs={{8,0},{10,2},{12,4},{14,6},{16,8},{18,10},{20,12},{22,14},{24,16},... | collective-permute-start | bytes 1966088 | tf_op jit(solution)/shard_map/ppermute | solution.py:236
  149.0 49.5 %collective-permute-start.22 = (bf16[512,640]{1,0:T(8,128)(2,1)}, bf16[512,640]{1,0:T(8,128)(2,1)}, u32[]{:S(2)}, u32[]{:S(2)}) collective-permute-start(bf16[512,640]{1,0:T(8,128)(2,1)} %collective-permute-done.18.rest_5_), channel_id=1, source_target_pairs={{0,8},{2,10},{4,12},{6,14},{8,16},{10,18},{12,20},{14,22},{16,24},... | collective-permute-start | bytes 1966088 | tf_op jit(solution)/shard_map/ppermute | solution.py:236
  163.1 37.2 %collective-permute-start.21 = (bf16[512,640]{1,0:T(8,128)(2,1)}, bf16[512,640]{1,0:T(8,128)(2,1)}, u32[]{:S(2)}, u32[]{:S(2)}) collective-permute-start(bf16[512,640]{1,0:T(8,128)(2,1)} %broadcast_select_fusion.1), channel_id=1, source_target_pairs={{0,2},{2,0},{4,6},{6,4},{8,10},{10,8},{12,14},{14,12},{16,18},{18,... | collective-permute-start | bytes 1966088 | tf_op jit(solution)/shard_map/ppermute | solution.py:241
  227.4 51.4 %collective-permute-start.56 = (bf16[512,640]{1,0:T(8,128)(2,1)}, bf16[512,640]{1,0:T(8,128)(2,1)}, u32[]{:S(2)}, u32[]{:S(2)}) collective-permute-start(bf16[512,640]{1,0:T(8,128)(2,1)} %get-tuple-element.99), channel_id=1, source_target_pairs={{0,2},{2,0},{4,6},{6,4},{8,10},{10,8},{12,14},{14,12},{16,18},{18,... | collective-permute-start | bytes 1966088 | tf_op jit(solution)/shard_map/ppermute | solution.py:241
  228.0 52.4 %collective-permute-start.57 = (bf16[512,640]{1,0:T(8,128)(2,1)}, bf16[512,640]{1,0:T(8,128)(2,1)}, u32[]{:S(2)}, u32[]{:S(2)}) collective-permute-start(bf16[512,640]{1,0:T(8,128)(2,1)} %get-tuple-element.101), channel_id=1, source_target_pairs={{0,2},{2,0},{4,6},{6,4},{8,10},{10,8},{12,14},{14,12},{16,18},{18,... | collective-permute-start | bytes 1966088 | tf_op jit(solution)/shard_map/ppermute | solution.py:241
  229.4 52.9 %collective-permute-start.59 = (bf16[512,640]{1,0:T(8,128)(2,1)}, bf16[512,640]{1,0:T(8,128)(2,1)}, u32[]{:S(2)}, u32[]{:S(2)}) collective-permute-start(bf16[512,640]{1,0:T(8,128)(2,1)} %get-tuple-element.103), channel_id=1, source_target_pairs={{8,0},{10,2},{12,4},{14,6},{16,8},{18,10},{20,12},{22,14},{24,16},... | collective-permute-start | bytes 1966088 | tf_op jit(solution)/shard_map/ppermute | solution.py:236
  232.3 50.7 %collective-permute-start.62 = (bf16[512,640]{1,0:T(8,128)(2,1)}, bf16[512,640]{1,0:T(8,128)(2,1)}, u32[]{:S(2)}, u32[]{:S(2)}) collective-permute-start(bf16[512,640]{1,0:T(8,128)(2,1)} %get-tuple-element.106), channel_id=1, source_target_pairs={{0,8},{2,10},{4,12},{6,14},{8,16},{10,18},{12,20},{14,22},{16,24},... | collective-permute-start | bytes 1966088 | tf_op jit(solution)/shard_map/ppermute | solution.py:236
  252.0 35.2 %collective-permute-start.48 = (bf16[512,640]{1,0:T(8,128)(2,1)}, bf16[512,640]{1,0:T(8,128)(2,1)}, u32[]{:S(2)}, u32[]{:S(2)}) collective-permute-start(bf16[512,640]{1,0:T(8,128)(2,1)} %get-tuple-element.90), channel_id=1, source_target_pairs={{0,2},{2,0},{4,6},{6,4},{8,10},{10,8},{12,14},{14,12},{16,18},{18,... | collective-permute-start | bytes 1966088 | tf_op jit(solution)/shard_map/ppermute | solution.py:241
  278.8 17.7 %collective-permute-start.49 = (bf16[512,640]{1,0:T(8,128)(2,1)S(1)}, bf16[512,640]{1,0:T(8,128)(2,1)S(1)}, u32[]{:S(2)}, u32[]{:S(2)}) collective-permute-start(bf16[512,640]{1,0:T(8,128)(2,1)S(1)} %copy-done.87), channel_id=1, source_target_pairs={{0,2},{2,0},{4,6},{6,4},{8,10},{10,8},{12,14},{14,12},{16,18},{18,... | collective-permute-start | bytes 1966088 | tf_op jit(solution)/shard_map/ppermute | solution.py:241
  280.4 18.2 %collective-permute-start.51 = (bf16[512,640]{1,0:T(8,128)(2,1)S(1)}, bf16[512,640]{1,0:T(8,128)(2,1)S(1)}, u32[]{:S(2)}, u32[]{:S(2)}) collective-permute-start(bf16[512,640]{1,0:T(8,128)(2,1)S(1)} %copy-done.85), channel_id=1, source_target_pairs={{8,0},{10,2},{12,4},{14,6},{16,8},{18,10},{20,12},{22,14},{24,16},... | collective-permute-start | bytes 1966088 | tf_op jit(solution)/shard_map/ppermute | solution.py:236
  282.4 28.2 %collective-permute-start.41 = (bf16[512,640]{1,0:T(8,128)(2,1)S(1)}, bf16[512,640]{1,0:T(8,128)(2,1)S(1)}, u32[]{:S(2)}, u32[]{:S(2)}) collective-permute-start(bf16[512,640]{1,0:T(8,128)(2,1)S(1)} %copy-done.89), channel_id=1, source_target_pairs={{0,2},{2,0},{4,6},{6,4},{8,10},{10,8},{12,14},{14,12},{16,18},{18,... | collective-permute-start | bytes 1966088 | tf_op jit(solution)/shard_map/ppermute | solution.py:241
  283.0 39.4 %collective-permute-start.33 = (bf16[512,640]{1,0:T(8,128)(2,1)}, bf16[512,640]{1,0:T(8,128)(2,1)S(1)}, u32[]{:S(2)}, u32[]{:S(2)}) collective-permute-start(bf16[512,640]{1,0:T(8,128)(2,1)} %get-tuple-element.74), channel_id=1, source_target_pairs={{0,2},{2,0},{4,6},{6,4},{8,10},{10,8},{12,14},{14,12},{16,18},{18,... | collective-permute-start | bytes 1966088 | tf_op jit(solution)/shard_map/ppermute | solution.py:241
  287.3 37.3 %collective-permute-start.54 = (bf16[512,640]{1,0:T(8,128)(2,1)S(1)}, bf16[512,640]{1,0:T(8,128)(2,1)S(1)}, u32[]{:S(2)}, u32[]{:S(2)}) collective-permute-start(bf16[512,640]{1,0:T(8,128)(2,1)S(1)} %copy-done.81), channel_id=1, source_target_pairs={{0,8},{2,10},{4,12},{6,14},{8,16},{10,18},{12,20},{14,22},{16,24},... | collective-permute-start | bytes 1966088 | tf_op jit(solution)/shard_map/ppermute | solution.py:236
  296.5 30.1 %collective-permute-start.43 = (bf16[512,640]{1,0:T(8,128)(2,1)S(1)}, bf16[512,640]{1,0:T(8,128)(2,1)S(1)}, u32[]{:S(2)}, u32[]{:S(2)}) collective-permute-start(bf16[512,640]{1,0:T(8,128)(2,1)S(1)} %copy-done.83), channel_id=1, source_target_pairs={{8,0},{10,2},{12,4},{14,6},{16,8},{18,10},{20,12},{22,14},{24,16},... | collective-permute-start | bytes 1966088 | tf_op jit(solution)/shard_map/ppermute | solution.py:236
  298.5 32.0 %collective-permute-start.60 = (bf16[512,640]{1,0:T(8,128)(2,1)S(1)}, bf16[512,640]{1,0:T(8,128)(2,1)S(1)}, u32[]{:S(2)}, u32[]{:S(2)}) collective-permute-start(bf16[512,640]{1,0:T(8,128)(2,1)S(1)} %get-tuple-element.136), channel_id=1, source_target_pairs={{0,4},{2,6},{4,0},{6,2},{8,12},{10,14},{12,8},{14,10},{16,20},{18,... | collective-permute-start | bytes 1966088 | tf_op jit(solution)/shard_map/ppermute | solution.py:241
  310.6 22.4 %collective-permute-start.46 = (bf16[512,640]{1,0:T(8,128)(2,1)S(1)}, bf16[512,640]{1,0:T(8,128)(2,1)S(1)}, u32[]{:S(2)}, u32[]{:S(2)}) collective-permute-start(bf16[512,640]{1,0:T(8,128)(2,1)S(1)} %get-tuple-element.88), channel_id=1, source_target_pairs={{0,8},{2,10},{4,12},{6,14},{8,16},{10,18},{12,20},{14,22},{16,24},... | collective-permute-start | bytes 1966088 | tf_op jit(solution)/shard_map/ppermute | solution.py:236
  322.4 17.7 %collective-permute-start.52 = (bf16[512,640]{1,0:T(8,128)(2,1)S(1)}, bf16[512,640]{1,0:T(8,128)(2,1)S(1)}, u32[]{:S(2)}, u32[]{:S(2)}) collective-permute-start(bf16[512,640]{1,0:T(8,128)(2,1)S(1)} %get-tuple-element.132), channel_id=1, source_target_pairs={{0,4},{2,6},{4,0},{6,2},{8,12},{10,14},{12,8},{14,10},{16,20},{18,... | collective-permute-start | bytes 1966088 | tf_op jit(solution)/shard_map/ppermute | solution.py:241
  324.6 17.5 %collective-permute-start.35 = (bf16[512,640]{1,0:T(8,128)(2,1)S(1)}, bf16[512,640]{1,0:T(8,128)(2,1)S(1)}, u32[]{:S(2)}, u32[]{:S(2)}) collective-permute-start(bf16[512,640]{1,0:T(8,128)(2,1)S(1)} %get-tuple-element.76), channel_id=1, source_target_pairs={{8,0},{10,2},{12,4},{14,6},{16,8},{18,10},{20,12},{22,14},{24,16},... | collective-permute-start | bytes 1966088 | tf_op jit(solution)/shard_map/ppermute | solution.py:236
  326.6 16.2 %collective-permute-start.38 = (bf16[512,640]{1,0:T(8,128)(2,1)S(1)}, bf16[512,640]{1,0:T(8,128)(2,1)S(1)}, u32[]{:S(2)}, u32[]{:S(2)}) collective-permute-start(bf16[512,640]{1,0:T(8,128)(2,1)S(1)} %get-tuple-element.79), channel_id=1, source_target_pairs={{0,8},{2,10},{4,12},{6,14},{8,16},{10,18},{12,20},{14,22},{16,24},... | collective-permute-start | bytes 1966088 | tf_op jit(solution)/shard_map/ppermute | solution.py:236
  330.5 23.6 %collective-permute-start.44 = (bf16[512,640]{1,0:T(8,128)(2,1)S(1)}, bf16[512,640]{1,0:T(8,128)(2,1)S(1)}, u32[]{:S(2)}, u32[]{:S(2)}) collective-permute-start(bf16[512,640]{1,0:T(8,128)(2,1)S(1)} %get-tuple-element.128), channel_id=1, source_target_pairs={{0,4},{2,6},{4,0},{6,2},{8,12},{10,14},{12,8},{14,10},{16,20},{18,... | collective-permute-start | bytes 1966088 | tf_op jit(solution)/shard_map/ppermute | solution.py:241
  333.0 35.1 %collective-permute-start.58 = (bf16[512,640]{1,0:T(8,128)(2,1)S(1)}, bf16[512,640]{1,0:T(8,128)(2,1)S(1)}, u32[]{:S(2)}, u32[]{:S(2)}) collective-permute-start(bf16[512,640]{1,0:T(8,128)(2,1)S(1)} %get-tuple-element.135), channel_id=1, source_target_pairs={{0,4},{2,6},{4,0},{6,2},{8,12},{10,14},{12,8},{14,10},{16,20},{18,... | collective-permute-start | bytes 1966088 | tf_op jit(solution)/shard_map/ppermute | solution.py:241
  340.0 42.1 %collective-permute-start.36 = (bf16[512,640]{1,0:T(8,128)(2,1)S(1)}, bf16[512,640]{1,0:T(8,128)(2,1)S(1)}, u32[]{:S(2)}, u32[]{:S(2)}) collective-permute-start(bf16[512,640]{1,0:T(8,128)(2,1)S(1)} %get-tuple-element.124), channel_id=1, source_target_pairs={{0,4},{2,6},{4,0},{6,2},{8,12},{10,14},{12,8},{14,10},{16,20},{18,... | collective-permute-start | bytes 1966088 | tf_op jit(solution)/shard_map/ppermute | solution.py:241
  342.1 51.0 %collective-permute-start.50 = (bf16[512,640]{1,0:T(8,128)(2,1)S(1)}, bf16[512,640]{1,0:T(8,128)(2,1)S(1)}, u32[]{:S(2)}, u32[]{:S(2)}) collective-permute-start(bf16[512,640]{1,0:T(8,128)(2,1)S(1)} %get-tuple-element.131), channel_id=1, source_target_pairs={{0,4},{2,6},{4,0},{6,2},{8,12},{10,14},{12,8},{14,10},{16,20},{18,... | collective-permute-start | bytes 1966088 | tf_op jit(solution)/shard_map/ppermute | solution.py:241
  342.8 51.8 %collective-permute-start.61 = (bf16[512,640]{1,0:T(8,128)(2,1)S(1)}, bf16[512,640]{1,0:T(8,128)(2,1)S(1)}, u32[]{:S(2)}, u32[]{:S(2)}) collective-permute-start(bf16[512,640]{1,0:T(8,128)(2,1)S(1)} %get-tuple-element.137), channel_id=1, source_target_pairs={{8,0},{10,2},{12,4},{14,6},{16,8},{18,10},{20,12},{22,14},{24,16},... | collective-permute-start | bytes 1966088 | tf_op jit(solution)/shard_map/ppermute | solution.py:236
  354.1 42.0 %collective-permute-start.63 = (bf16[512,640]{1,0:T(8,128)(2,1)S(1)}, bf16[512,640]{1,0:T(8,128)(2,1)S(1)}, u32[]{:S(2)}, u32[]{:S(2)}) collective-permute-start(bf16[512,640]{1,0:T(8,128)(2,1)S(1)} %get-tuple-element.138), channel_id=1, source_target_pairs={{0,8},{2,10},{4,12},{6,14},{8,16},{10,18},{12,20},{14,22},{16,24},... | collective-permute-start | bytes 1966088 | tf_op jit(solution)/shard_map/ppermute | solution.py:236
  368.1 31.7 %collective-permute-start.53 = (bf16[512,640]{1,0:T(8,128)(2,1)S(1)}, bf16[512,640]{1,0:T(8,128)(2,1)S(1)}, u32[]{:S(2)}, u32[]{:S(2)}) collective-permute-start(bf16[512,640]{1,0:T(8,128)(2,1)S(1)} %get-tuple-element.133), channel_id=1, source_target_pairs={{8,0},{10,2},{12,4},{14,6},{16,8},{18,10},{20,12},{22,14},{24,16},... | collective-permute-start | bytes 1966088 | tf_op jit(solution)/shard_map/ppermute | solution.py:236
  382.2 21.8 %collective-permute-start.55 = (bf16[512,640]{1,0:T(8,128)(2,1)S(1)}, bf16[512,640]{1,0:T(8,128)(2,1)S(1)}, u32[]{:S(2)}, u32[]{:S(2)}) collective-permute-start(bf16[512,640]{1,0:T(8,128)(2,1)S(1)} %get-tuple-element.134), channel_id=1, source_target_pairs={{0,8},{2,10},{4,12},{6,14},{8,16},{10,18},{12,20},{14,22},{16,24},... | collective-permute-start | bytes 1966088 | tf_op jit(solution)/shard_map/ppermute | solution.py:236
  393.0 17.7 %collective-permute-start.40 = (bf16[512,640]{1,0:T(8,128)(2,1)S(1)}, bf16[512,640]{1,0:T(8,128)(2,1)S(1)}, u32[]{:S(2)}, u32[]{:S(2)}) collective-permute-start(bf16[512,640]{1,0:T(8,128)(2,1)S(1)} %copy-done.79), channel_id=1, source_target_pairs={{0,2},{2,0},{4,6},{6,4},{8,10},{10,8},{12,14},{14,12},{16,18},{18,... | collective-permute-start | bytes 1966088 | tf_op jit(solution)/shard_map/ppermute | solution.py:241
  394.6 17.5 %collective-permute-start.42 = (bf16[512,640]{1,0:T(8,128)(2,1)S(1)}, bf16[512,640]{1,0:T(8,128)(2,1)S(1)}, u32[]{:S(2)}, u32[]{:S(2)}) collective-permute-start(bf16[512,640]{1,0:T(8,128)(2,1)S(1)} %get-tuple-element.127), channel_id=1, source_target_pairs={{0,4},{2,6},{4,0},{6,2},{8,12},{10,14},{12,8},{14,10},{16,20},{18,... | collective-permute-start | bytes 1966088 | tf_op jit(solution)/shard_map/ppermute | solution.py:241
  396.1 18.1 %collective-permute-start.45 = (bf16[512,640]{1,0:T(8,128)(2,1)S(1)}, bf16[512,640]{1,0:T(8,128)(2,1)S(1)}, u32[]{:S(2)}, u32[]{:S(2)}) collective-permute-start(bf16[512,640]{1,0:T(8,128)(2,1)S(1)} %get-tuple-element.129), channel_id=1, source_target_pairs={{8,0},{10,2},{12,4},{14,6},{16,8},{18,10},{20,12},{22,14},{24,16},... | collective-permute-start | bytes 1966088 | tf_op jit(solution)/shard_map/ppermute | solution.py:236
  399.8 19.2 %collective-permute-start.47 = (bf16[512,640]{1,0:T(8,128)(2,1)S(1)}, bf16[512,640]{1,0:T(8,128)(2,1)S(1)}, u32[]{:S(2)}, u32[]{:S(2)}) collective-permute-start(bf16[512,640]{1,0:T(8,128)(2,1)S(1)} %get-tuple-element.130), channel_id=1, source_target_pairs={{0,8},{2,10},{4,12},{6,14},{8,16},{10,18},{12,20},{14,22},{16,24},... | collective-permute-start | bytes 1966088 | tf_op jit(solution)/shard_map/ppermute | solution.py:236
  404.0 16.7 %collective-permute-start.32 = (bf16[512,640]{1,0:T(8,128)(2,1)S(1)}, bf16[512,640]{1,0:T(8,128)(2,1)S(1)}, u32[]{:S(2)}, u32[]{:S(2)}) collective-permute-start(bf16[512,640]{1,0:T(8,128)(2,1)S(1)} %get-tuple-element.72), channel_id=1, source_target_pairs={{0,2},{2,0},{4,6},{6,4},{8,10},{10,8},{12,14},{14,12},{16,18},{18,... | collective-permute-start | bytes 1966088 | tf_op jit(solution)/shard_map/ppermute | solution.py:241
  410.7 11.1 %collective-permute-start.34 = (bf16[512,640]{1,0:T(8,128)(2,1)S(1)}, bf16[512,640]{1,0:T(8,128)(2,1)S(1)}, u32[]{:S(2)}, u32[]{:S(2)}) collective-permute-start(bf16[512,640]{1,0:T(8,128)(2,1)S(1)} %get-tuple-element.123), channel_id=1, source_target_pairs={{0,4},{2,6},{4,0},{6,2},{8,12},{10,14},{12,8},{14,10},{16,20},{18,... | collective-permute-start | bytes 1966088 | tf_op jit(solution)/shard_map/ppermute | solution.py:241
  412.2 12.7 %collective-permute-start.37 = (bf16[512,640]{1,0:T(8,128)(2,1)S(1)}, bf16[512,640]{1,0:T(8,128)(2,1)S(1)}, u32[]{:S(2)}, u32[]{:S(2)}) collective-permute-start(bf16[512,640]{1,0:T(8,128)(2,1)S(1)} %get-tuple-element.125), channel_id=1, source_target_pairs={{8,0},{10,2},{12,4},{14,6},{16,8},{18,10},{20,12},{22,14},{24,16},... | collective-permute-start | bytes 1966088 | tf_op jit(solution)/shard_map/ppermute | solution.py:236
  414.2 14.7 %collective-permute-start.39 = (bf16[512,640]{1,0:T(8,128)(2,1)S(1)}, bf16[512,640]{1,0:T(8,128)(2,1)S(1)}, u32[]{:S(2)}, u32[]{:S(2)}) collective-permute-start(bf16[512,640]{1,0:T(8,128)(2,1)S(1)} %get-tuple-element.126), channel_id=1, source_target_pairs={{0,8},{2,10},{4,12},{6,14},{8,16},{10,18},{12,20},{14,22},{16,24},... | collective-permute-start | bytes 1966088 | tf_op jit(solution)/shard_map/ppermute | solution.py:236
  (92 other events, 1024.8 us)

commit v2 on v1

--- a/solution.py
+++ b/solution.py
@@ -230,55 +230,341 @@
     )(where, queries, policy, ref, attn, probs, inv, *pool)
 
 
-def shift(value, steps):
-    count = lax.axis_size("frame")
-    pairs = [(s, s + steps) for s in range(count) if 0 <= s + steps < count]
-    return lax.ppermute(value, "frame", pairs)
-
-
-def swap(value, bit):
-    count = lax.axis_size("frame")
-    return lax.ppermute(value, "frame", [(s, s ^ bit) for s in range(count)])
-
-
-def add(*terms):
-    total = terms[0].astype(jnp.float32)
-    for term in terms[1:]:
-        total = total + term.astype(jnp.float32)
-    return total.astype(jnp.bfloat16)
-
-
-def gather(kv, corner, upper, levels):
-    far = [(shift(kv, 4), shift(kv, -4))]
-    across, along = swap(kv, 1), swap(kv, 2)
-    for level in range(3, levels):
-        step = 1 << (level - 1)
-        far.append((shift(far[-1][0], step), shift(far[-1][1], -step)))
-    cross = swap(jnp.where(upper, far[0][0], far[0][1]), 2)
-    diagonal = swap(jnp.where(corner, along, cross), 1)
-    return [kv, across, along, cross, diagonal] + [x for pair in far for x in pair]
-
-
-def scatter(parts, corner, upper, levels):
-    own, across, along, cross, diagonal = parts[:5]
-    before, after = list(parts[5::2]), list(parts[6::2])
-    zero = jnp.zeros((), jnp.bfloat16)
-    diagonal = swap(diagonal, 1)
-    across = swap(across, 1)
-    for level in range(levels - 1, 2, -1):
-        step = 1 << (level - 1)
-        n = level - 2
-        back, forth = shift(before[n], -step), shift(after[n], step)
-        if n > 1:
-            before[n - 1], after[n - 1] = add(before[n - 1], back), add(after[n - 1], forth)
-        else:
-            extra = (back, forth)
-    cross = swap(add(cross, jnp.where(corner, zero, diagonal)), 2)
-    along = swap(add(along, jnp.where(corner, diagonal, zero)), 2)
-    more = extra if levels > 3 else (zero, zero)
-    first = add(before[0], more[0], jnp.where(upper, cross, zero))
-    second = add(after[0], more[1], jnp.where(upper, zero, cross))
-    return add(own, across, along, shift(first, -4), shift(second, 4))
+MESH = pl.DeviceIdType.MESH
+PIECE = 64
+STRIP = 16
+
+
+class Place:
+    def __init__(self, count):
+        me = lax.axis_index("frame")
+        self.count = count
+        self.me = me
+        self.x = me + 1 - 2 * (me % 2)
+        self.y = me + 2 - 4 * ((me // 2) % 2)
+        at = me % 4
+        self.corner = (at == 0) | (at == 3)
+        self.inner = jnp.logical_not(self.corner)
+        self.upper = at >= 2
+        self.lower = at < 2
+        low, high = me >= 4, me + 4 < count
+        self.has_cross = (self.lower & low) | (self.upper & high)
+        self.gives_cross = (self.upper & low) | (self.lower & high)
+
+
+def mover(send, recv, rows_of):
+    def move(src, dst, n, p, target):
+        rows = rows_of(p)
+        return pltpu.make_async_remote_copy(
+            src_ref=src.at[rows],
+            dst_ref=dst.at[rows],
+            send_sem=send.at[n, p],
+            recv_sem=recv.at[n, p],
+            device_id={"frame": target},
+            device_id_type=MESH,
+        )
+
+    return move
+
+
+def rows_of(p):
+    return pl.ds(pl.multiple_of(p * PIECE, PIECE), PIECE)
+
+
+def both(a, b):
+    return jnp.logical_and(a, b)
+
+
+def gather_kernel(count, levels, pieces, kv, *rest):
+    outs, (send, recv) = rest[:-2], rest[-2:]
+    x, y, cross, diagonal = outs[:4]
+    at = Place(count)
+    me = at.me
+    move = mover(send, recv, rows_of)
+
+    def before(level):
+        return 2 * level
+
+    def after(level):
+        return 2 * level + 1
+
+    @pl.loop(0, pieces)
+    def _(p):
+        @pl.when(me + 4 < count)
+        def _():
+            move(kv, outs[4], 4, p, me + 4).start()
+
+        @pl.when(me >= 4)
+        def _():
+            move(kv, outs[5], 5, p, me - 4).start()
+
+        move(kv, y, 1, p, at.y).start()
+        move(kv, x, 0, p, at.x).start()
+
+    for level in range(2, levels):
+        step = 1 << level
+        b, a = before(level), after(level)
+
+        @pl.loop(0, pieces)
+        def _(p):
+            @pl.when(me >= step)
+            def _():
+                move(kv, outs[b], b, p, at.x).wait_recv()
+                if level + 1 < levels:
+
+                    @pl.when(me + step < count)
+                    def _():
+                        move(outs[b], outs[b + 2], b + 2, p, me + step).start()
+
+                if level == 2:
+
+                    @pl.when(at.upper)
+                    def _():
+                        move(outs[b], cross, 2, p, at.y).start()
+
+            @pl.when(me + step < count)
+            def _():
+                move(kv, outs[a], a, p, at.x).wait_recv()
+                if level + 1 < levels:
+
+                    @pl.when(me >= step)
+                    def _():
+                        move(outs[a], outs[a + 2], a + 2, p, me - step).start()
+
+                if level == 2:
+
+                    @pl.when(at.lower)
+                    def _():
+                        move(outs[a], cross, 2, p, at.y).start()
+
+            if level == 2:
+                move(kv, y, 1, p, at.x).wait_recv()
+
+                @pl.when(at.corner)
+                def _():
+                    move(y, diagonal, 3, p, at.x).start()
+
+        if level == 2:
+
+            @pl.loop(0, pieces)
+            def _(p):
+                @pl.when(at.has_cross)
+                def _():
+                    move(kv, cross, 2, p, at.x).wait_recv()
+
+                    @pl.when(at.inner)
+                    def _():
+                        move(cross, diagonal, 3, p, at.x).start()
+
+    @pl.loop(0, pieces)
+    def _(p):
+        move(kv, x, 0, p, at.x).wait_recv()
+        move(kv, x, 0, p, at.x).wait_send()
+        move(kv, y, 1, p, at.x).wait_send()
+
+        @pl.when(at.inner | at.has_cross)
+        def _():
+            move(kv, diagonal, 3, p, at.x).wait_recv()
+
+        @pl.when(at.corner | at.has_cross)
+        def _():
+            move(kv, diagonal, 3, p, at.x).wait_send()
+
+        @pl.when(at.gives_cross)
+        def _():
+            move(kv, cross, 2, p, at.x).wait_send()
+
+        for level in range(2, levels):
+            step = 1 << (level - 1) if level > 2 else 4
+            start = step if level > 2 else 0
+            b, a = before(level), after(level)
+
+            @pl.when(both(me >= start, me + step < count))
+            def _():
+                move(kv, outs[b], b, p, at.x).wait_send()
+
+            @pl.when(both(me + start < count, me >= step))
+            def _():
+                move(kv, outs[a], a, p, at.x).wait_send()
+
+
+def scatter_kernel(count, levels, pieces, *refs):
+    n = 2 * levels
+    parts, out = refs[: n + 1], refs[n + 1]
+    held, land, send, recv, local_sems, out_sems = refs[n + 2 :]
+    own, parts = parts[0], parts[1:]
+    at = Place(count)
+    me = at.me
+    move = mover(send, recv, rows_of)
+    kept = [n, 1, 2] + list(range(4, n - 2))
+
+    def bring(slot):
+        return pltpu.make_async_copy(
+            own if slot == n else parts[slot], held.at[slot], local_sems.at[slot]
+        )
+
+    def leave(p):
+        return pltpu.make_async_copy(held.at[n, rows_of(p)], out.at[rows_of(p)], out_sems.at[p])
+
+    def add_to(slot, others, p):
+        for j in range(PIECE // STRIP):
+            rows = pl.ds(pl.multiple_of(p * PIECE + j * STRIP, STRIP), STRIP)
+            total = held[slot, rows, :].astype(jnp.float32)
+            for other in others:
+                total = total + land[other, rows, :].astype(jnp.float32)
+            held[slot, rows, :] = total.astype(jnp.bfloat16)
+
+    for slot in kept:
+        bring(slot).start()
+
+    top_b, top_a = n - 2, n - 1
+    reach, hop = 1 << (levels - 1), 1 << (levels - 2)
+
+    @pl.loop(0, pieces)
+    def _(p):
+        move(parts[3], land.at[3], 3, p, at.x).start()
+        if levels > 3:
+
+            @pl.when(me >= reach)
+            def _():
+                move(parts[top_b], land.at[top_b], top_b, p, me - hop).start()
+
+            @pl.when(me + reach < count)
+            def _():
+                move(parts[top_a], land.at[top_a], top_a, p, me + hop).start()
+
+    @pl.loop(0, pieces)
+    def _(p):
+        move(parts[0], land.at[0], 0, p, at.x).start()
+
+    for slot in kept:
+        bring(slot).wait()
+
+    @pl.loop(0, pieces)
+    def _(p):
+        move(own, land.at[3], 3, p, at.x).wait_recv()
+
+        @pl.when(at.corner)
+        def _():
+            add_to(1, [3], p)
+
+        @pl.when(at.inner)
+        def _():
+            add_to(2, [3], p)
+
+        move(held.at[2], land.at[2], 2, p, at.y).start()
+        move(held.at[1], land.at[1], 1, p, at.y).start()
+
+    for level in range(levels - 2, 1, -1):
+        b, a = 2 * level, 2 * level + 1
+        step = 1 << level
+        back = 4 if level == 2 else step // 2
+
+        @pl.loop(0, pieces)
+        def _(p):
+            @pl.when(both(me >= step, me + step < count))
+            def _():
+                move(own, land.at[b + 2], b + 2, p, at.x).wait_recv()
+                add_to(b, [b + 2], p)
+
+            @pl.when(both(me >= step, me + step < count))
+            def _():
+                move(own, land.at[a + 2], a + 2, p, at.x).wait_recv()
+                add_to(a, [a + 2], p)
+
+            if level == 2:
+                move(own, land.at[2], 2, p, at.x).wait_recv()
+
+                @pl.when(at.upper)
+                def _():
+                    add_to(4, [2], p)
+
+                @pl.when(at.lower)
+                def _():
+                    add_to(5, [2], p)
+
+            @pl.when(me >= step)
+            def _():
+                move(held.at[b], land.at[b], b, p, me - back).start()
+
+            @pl.when(me + step < count)
+            def _():
+                move(held.at[a], land.at[a], a, p, me + back).start()
+
+    @pl.loop(0, pieces)
+    def _(p):
+        move(own, land.at[0], 0, p, at.x).wait_recv()
+        move(own, land.at[1], 1, p, at.x).wait_recv()
+        add_to(n, [0, 1], p)
+
+        @pl.when(me + 4 < count)
+        def _():
+            move(own, land.at[4], 4, p, at.x).wait_recv()
+            add_to(n, [4], p)
+
+        @pl.when(me >= 4)
+        def _():
+            move(own, land.at[5], 5, p, at.x).wait_recv()
+            add_to(n, [5], p)
+
+        leave(p).start()
+
+    @pl.loop(0, pieces)
+    def _(p):
+        for slot in range(4):
+            move(own, land.at[slot], slot, p, at.x).wait_send()
+        for level in range(2, levels):
+            b, a = 2 * level, 2 * level + 1
+
+            @pl.when(me >= (1 << level))
+            def _():
+                move(own, land.at[b], b, p, at.x).wait_send()
+
+            @pl.when(me + (1 << level) < count)
+            def _():
+                move(own, land.at[a], a, p, at.x).wait_send()
+
+        leave(p).wait()
+
+
+def gather(kv, levels):
+    n, pieces = 2 * levels, kv.shape[0] // PIECE
+    anywhere = pl.BlockSpec(memory_space=pl.ANY)
+    return [kv] + list(
+        pl.pallas_call(
+            functools.partial(gather_kernel, lax.axis_size("frame"), levels, pieces),
+            in_specs=[anywhere],
+            out_specs=[anywhere] * n,
+            out_shape=[jax.ShapeDtypeStruct(kv.shape, kv.dtype)] * n,
+            scratch_shapes=[pltpu.SemaphoreType.DMA((n, pieces))] * 2,
+            compiler_params=pltpu.CompilerParams(has_side_effects=True),
+            name="gather",
+        )(kv)
+    )
+
+
+def scatter(parts, levels):
+    n, pieces = 2 * levels, parts[0].shape[0] // PIECE
+    shape = parts[0].shape
+    anywhere = pl.BlockSpec(memory_space=pl.ANY)
+    return pl.pallas_call(
+        functools.partial(scatter_kernel, lax.axis_size("frame"), levels, pieces),
+        in_specs=[anywhere] * (n + 1),
+        out_specs=anywhere,
+        out_shape=jax.ShapeDtypeStruct(shape, jnp.bfloat16),
+        scratch_shapes=[
+            pltpu.VMEM((n + 1,) + shape, jnp.bfloat16),
+            pltpu.VMEM((n,) + shape, jnp.bfloat16),
+            pltpu.SemaphoreType.DMA((n, pieces)),
+            pltpu.SemaphoreType.DMA((n, pieces)),
+            pltpu.SemaphoreType.DMA((n + 1,)),
+            pltpu.SemaphoreType.DMA((pieces,)),
+        ],
+        compiler_params=pltpu.CompilerParams(
+            has_side_effects=True, vmem_limit_bytes=56 * 1024 * 1024
+        ),
+        name="scatter",
+    )(*parts)
 
 
 def places(gap, me, levels):
@@ -298,13 +584,6 @@
     return at
 
 
-def chunk_count(heads):
-    for n in (4, 2):
-        if heads % n == 0:
-            return n
-    return 1
-
-
 def local(queries, keys, values, policy_grad, ref_velocity, key_lists, frame_tokens):
     rows, cols = queries.shape
     heads = cols // HD
@@ -313,43 +592,22 @@
     levels = lax.axis_size("frame").bit_length() - 1
     all_features = cols * lax.axis_size("head")
     me = lax.axis_index("frame")
-    corner_of = me % 4
-    corner = (corner_of == 0) | (corner_of == 3)
-    upper = corner_of >= 2
     where = (places(key_lists // blocks - me, me, levels) * blocks + key_lists % blocks).reshape(-1)
     ids = jnp.arange(frame_tokens.shape[0], dtype=jnp.int32)
     counts = jnp.sum(
         jnp.where(key_lists.reshape(-1, 1) == ids[None, :], frame_tokens[None, :], 0), axis=-1
     ).astype(jnp.int32)
-    n_chunks = chunk_count(heads)
-    each = heads // n_chunks
-    wide = each * HD
-    pools, forwards = [], []
-    for c in range(n_chunks):
-        cut = slice(c * wide, (c + 1) * wide)
-        kv = jnp.concatenate([keys[:, cut], values[:, cut]], axis=0)
-        pools.append(gather(kv, corner, upper, levels))
-    for c in range(n_chunks):
-        forwards.append(
-            forward(
-                where, counts, queries, ref_velocity, pools[c], c * each, each, blocks, list_len
-            )
-        )
-    squares = sum(f[2] for f in forwards)
+    pool = gather(jnp.concatenate([keys, values], axis=0), levels)
+    attn, probs, squares = forward(
+        where, counts, queries, ref_velocity, pool, 0, heads, blocks, list_len
+    )
     kl = lax.psum(jnp.sum(squares, axis=-1), "head") / all_features
     inv = jnp.broadcast_to((1.0 / (1.0 + kl))[:, None], (rows, HD))
-    grad_q, grad_k, grad_v = [], [], []
-    for c in range(n_chunks):
-        attn, probs, _ = forwards[c]
-        dq, *parts = backward(
-            where, queries, policy_grad, ref_velocity, attn, probs, inv,
-            pools[c], c * each, each, blocks, list_len,
-        )
-        total = scatter(parts, corner, upper, levels)
-        grad_q.append(dq)
-        grad_k.append(total[:rows])
-        grad_v.append(total[rows:])
-    return tuple(jnp.concatenate(x, axis=1) for x in (grad_q, grad_k, grad_v))
+    grad_q, *parts = backward(
+        where, queries, policy_grad, ref_velocity, attn, probs, inv, pool, 0, heads, blocks, list_len
+    )
+    total = scatter(parts, levels)
+    return grad_q, total[:rows], total[rows:]
 
 
 def solution(mesh):

time: 436 us -> 354 us (0.81)
  Pallas kernels: 73.7 us -> 322 us
  waiting for transfers between devices: 165 us -> 0 us
  starting transfers between devices: 133 us -> 0 us
  other arithmetic: 22.1 us -> 1.76 us
  local copies, waits for them, and re-layouts: 33.6 us -> 24.1 us
    pallas_call x0 -> x2, Pallas kernels: none -> 263 us  [the longest x1 131 us: gather(): pl.pallas_call(functools.partial(gather_kernel, lax.axis_size('frame'), l...]
    ppermute x64 -> x0, waiting for transfers between devices: 165 us -> none  [the longest x32 125 us: swap(): return lax.ppermute(value, 'frame', [(s, s ^ bit) for s in range(count)])]
    ppermute x64 -> x0, starting transfers between devices: 133 us -> none  [the longest x32 92.4 us: shift(): return lax.ppermute(value, 'frame', pairs)]
    unnamed x184 -> x31, local copies, waits for them, and re-layouts: 31.2 us -> 19.7 us
    convert_element_type x12 -> x0, other arithmetic: 10.1 us -> none  [add(): return total.astype(jnp.bfloat16)]
    pallas_call x4 -> x1, Pallas kernels: 41.9 us -> 32.3 us  [backward(): pl.pallas_call(functools.partial(backward_kernel, n_pool, blocks, list_le...]
    select_n x8 -> x0, other arithmetic: 6.25 us -> none  [the longest x4 4.21 us: gather(): cross = swap(jnp.where(upper, far[0][0], far[0][1]), 2)]
    concatenate x7 -> x0, other arithmetic: 5.38 us -> none  [the longest x3 3.46 us: local(): return tuple((jnp.concatenate(x, axis=1) for x in (grad_q, grad_k, grad_v)))]
  transfers between devices with their start and end apart: 64 -> 0, of which waited for: 33 -> 0; matrix products, arithmetic and copies ran while one was open for 4% -> 0% of each run, Pallas kernels for 13% -> 0%
where the time goes in v2:
time: 354 us; the launch traced here: 351 us
  Pallas kernels  322 us (91%)
  local copies, waits for them, and re-layouts  24.1 us (7%)
    pallas_call x1, Pallas kernels, gather(): pl.pallas_call(functools.partial(gather_kernel, lax.axis_size('frame'), l...  131 us
    pallas_call x1, Pallas kernels, scatter(): pl.pallas_call(functools.partial(scatter_kernel, lax.axis_size('frame'),...  131 us
    pallas_call x1, Pallas kernels, backward(): pl.pallas_call(functools.partial(backward_kernel, n_pool, blocks, list_le...  32.3 us
    pallas_call x1, Pallas kernels, forward(): pl.pallas_call(functools.partial(forward_kernel, n_pool, blocks, list_len...  26.9 us
    unnamed x31, local copies, waits for them, and re-layouts  19.7 us

profile of v2, /device:TPU:16, one launch (start us, length us, event | category | flops | bytes accessed | tf_op | source)
XLA Modules:
  0.0 351.2 jit_solution(7207375926690066160)
XLA Ops:
  0.7 0.7 fusion.8
  1.4 0.1 reshape.13.where_ref
  1.5 0.8 eq.56
  2.2 0.0 copy-start.14
  2.2 0.9 select_reduce_fusion.count_ref
  3.2 1.4 constant_dynamic-update-slice_fusion.1
  4.6 0.0 copy-done.14
  4.6 0.1 constant_dynamic-update-slice_fusion.kv.rest_0_
  4.7 0.0 copy-start
  4.7 1.5 copy-done
  6.2 131.5 %gather.1 = (bf16[512,2560]{1,0:T(8,128)(2,1)}, bf16[512,2560]{1,0:T(8,128)(2,1)}, bf16[512,2560]{1,0:T(8,128)(2,1)}, bf16[512,2560]{1,0:T(8,128)(2,1)}, bf16[51...) custom-call(bf16[512,2560]{1,0:T(8,128)(2,1)} %copy-done), custom_call_target="tpu_custom_call" | custom-call | tf_op jit(solution)/shard_map/gather/pallas_call | solution.py:534
  137.7 0.0 copy-start.1
  137.7 1.7 copy-done.1
  139.4 0.0 copy-start.2
  139.4 1.7 copy-done.2
  141.2 0.0 copy-start.3
  141.2 1.7 copy-done.3
  142.9 0.0 copy-start.4
  142.9 1.3 copy-done.4
  144.2 0.0 copy-start.6
  144.2 1.3 copy-done.6
  145.6 0.0 copy-start.5
  145.6 0.0 copy-start.7
  145.6 26.9 %forward.1 = (f32[256,2560]{1,0:T(8,128)S(1)}, bf16[20,256,768]{2,1,0:T(8,128)(2,1)}, f32[256,128]{1,0:T(8,128)S(1)}) custom-call(s32[12]{0:T(128)S(1)} %reshape.13.where_ref, s32[12]{0:T(128)S(1)} %select_reduce_fusion.count_ref, bf16[256,2560]{1,0:T(8,128)(2,1)S(1)} %copy-done.4, bf16[256,2560]{1,0:T(8,128)(2,1)S(1)} %copy-done.6, ...), custom_call_target="tpu_custom_call" | custom-call | flops 2013265920 | bytes 36700160 | tf_op jit(solution)/shard_map/forward/pallas_call | solution.py:162
  172.5 0.0 copy-start.8
  172.5 1.6 copy-done.8
  174.1 0.1 reduce_sum.19
  174.2 2.5 psum.7
  176.7 0.1 broadcast_in_dim.63.inv_ref
  176.8 0.0 copy-done.5
  176.8 0.0 copy-done.7
  176.8 0.0 copy-start.13
  176.8 1.3 copy-done.13
  178.1 32.3 %backward.1 = (bf16[256,2560]{1,0:T(8,128)(2,1)}, bf16[512,2560]{1,0:T(8,128)(2,1)S(1)}, bf16[512,2560]{1,0:T(8,128)(2,1)S(1)}, bf16[512,2560]{1,0:T(8,128)(2,1)...) custom-call(s32[12]{0:T(128)S(1)} %reshape.13.where_ref, ...), custom_call_target="tpu_custom_call" | custom-call | flops 4026531840 | bytes 62914560 | tf_op jit(solution)/shard_map/backward/pallas_call | solution.py:199
  210.5 0.0 copy-start.9
  210.5 1.5 copy-done.9
  212.0 0.0 copy-start.10
  212.0 1.5 copy-done.10
  213.5 0.0 copy-start.11
  213.5 1.5 copy-done.11
  215.0 0.0 copy-start.12
  215.0 1.5 copy-done.12
  216.5 131.3 %scatter.1 = bf16[512,2560]{1,0:T(8,128)(2,1)} custom-call(bf16[512,2560]{1,0:T(8,128)(2,1)} %copy-done.9, bf16[512,2560]{1,0:T(8,128)(2,1)} %copy-done.10, bf16[512,2560]{1,0:T(8,128)(2,1)} %copy-done.11, bf16[512,2560]{1,0:T(8,128)(2,1)} %copy-done.12, bf16[512,2560]{1,0:T(8,128)(2,1)} %get-tuple-element.40.refs_4_, ...), custom_call_target="tpu_custom_call" | custom-call | tf_op jit(solution)/shard_map/scatter/pallas_call | solution.py:550
  347.8 3.4 fusion.9
  (1 shorter events, 0.0 us)
Async XLA Ops:
  2.2 2.4 copy-start.14
  4.7 1.5 copy-start
  137.7 1.7 copy-start.1
  139.4 1.7 copy-start.2
  141.2 1.7 copy-start.3
  142.9 1.3 copy-start.4
  144.2 1.3 copy-start.6
  145.6 31.2 %copy-start.5 = (bf16[256,2560]{1,0:T(8,128)(2,1)S(1)}, bf16[256,2560]{1,0:T(8,128)(2,1)}, u32[]{:S(2)}) copy-start(bf16[256,2560]{1,0:T(8,128)(2,1)} %q_ref.3) | copy-start | bytes 3932164
  145.6 31.2 %copy-start.7 = (bf16[256,2560]{1,0:T(8,128)(2,1)S(1)}, bf16[256,2560]{1,0:T(8,128)(2,1)}, u32[]{:S(2)}) copy-start(bf16[256,2560]{1,0:T(8,128)(2,1)} %ref_ref.3) | copy-start | bytes 3932164
  172.5 1.6 copy-start.8
  176.8 1.3 copy-start.13
  210.5 1.5 copy-start.9
  212.0 1.5 copy-start.10
  213.5 1.5 copy-start.11
  215.0 1.5 copy-start.12

commit v3 on v2

--- a/solution.py
+++ b/solution.py
@@ -11,7 +11,7 @@
 HD = 128
 BLK = 128
 KL_WEIGHT = 1.0
-VMEM = 40 * 1024 * 1024
+VMEM = 60 * 1024 * 1024
 
 NT = (((1,), (1,)), ((), ()))
 NN = (((1,), (0,)), ((), ()))
@@ -231,7 +231,7 @@
 
 
 MESH = pl.DeviceIdType.MESH
-PIECE = 64
+PIECE = 32
 STRIP = 16
 
 
@@ -561,7 +561,7 @@
             pltpu.SemaphoreType.DMA((pieces,)),
         ],
         compiler_params=pltpu.CompilerParams(
-            has_side_effects=True, vmem_limit_bytes=56 * 1024 * 1024
+            has_side_effects=True, vmem_limit_bytes=VMEM
         ),
         name="scatter",
     )(*parts)

time: 354 us -> 340 us (0.960)
  local copies, waits for them, and re-layouts: 24.1 us -> 8.44 us
    unnamed x31 -> x5, local copies, waits for them, and re-layouts: 19.7 us -> 2.87 us
where the time goes in v3:
time: 340 us; the launch traced here: 337 us
  Pallas kernels  322 us (95%)
  local copies, waits for them, and re-layouts  8.44 us (2%)
    pallas_call x1, Pallas kernels, scatter(): pl.pallas_call(functools.partial(scatter_kernel, lax.axis_size('frame'),...  131 us
    pallas_call x1, Pallas kernels, gather(): pl.pallas_call(functools.partial(gather_kernel, lax.axis_size('frame'), l...  129 us
    pallas_call x1, Pallas kernels, backward(): pl.pallas_call(functools.partial(backward_kernel, n_pool, blocks, list_le...  34.4 us
    pallas_call x1, Pallas kernels, forward(): pl.pallas_call(functools.partial(forward_kernel, n_pool, blocks, list_len...  28.2 us

profile of v3, /device:TPU:16, one launch (start us, length us, event | category | flops | bytes accessed | tf_op | source)
XLA Modules:
  0.0 337.2 jit_solution(2595893836131500201)
XLA Ops:
  0.7 0.7 fusion.8
  1.4 0.6 reshape.13.where_ref
  2.0 0.8 eq.56
  2.7 0.0 copy-start.1
  2.7 1.5 select_reduce_fusion.count_ref
  4.2 1.4 constant_dynamic-update-slice_fusion.1
  5.6 0.0 copy-done.1
  5.6 0.1 constant_dynamic-update-slice_fusion.kv.rest_0_
  5.7 0.0 copy-start
  5.7 1.5 copy-done
  7.2 129.1 %gather.1 = (bf16[512,2560]{1,0:T(8,128)(2,1)}, bf16[512,2560]{1,0:T(8,128)(2,1)}, bf16[512,2560]{1,0:T(8,128)(2,1)}, bf16[512,2560]{1,0:T(8,128)(2,1)}, bf16[51...) custom-call(bf16[512,2560]{1,0:T(8,128)(2,1)} %copy-done), custom_call_target="tpu_custom_call" | custom-call | tf_op jit(solution)/shard_map/gather/pallas_call | solution.py:534
  136.3 28.2 %forward.1 = (f32[256,2560]{1,0:T(8,128)}, bf16[20,256,768]{2,1,0:T(8,128)(2,1)}, f32[256,128]{1,0:T(8,128)}) custom-call(s32[12]{0:T(128)} %reshape.13.where_ref, s32[12]{0:T(128)} %select_reduce_fusion.count_ref, bf16[256,2560]{1,0:T(8,128)(2,1)} %q_ref.3, bf16[256,2560]{1,0:T(8,128)(2,1)} %ref_ref.3, bf16[512,2560]{1,0:T(8,128)(2,1)} %copy-done, ...), custom_call_target="tpu_custom_call" | custom-call | flops 2013265920 | bytes 36700160 | tf_op jit(solution)/shard_map/forward/pallas_call | solution.py:162
  164.5 1.0 reduce_sum.19
  165.5 2.5 psum.7
  168.0 0.8 broadcast_in_dim.63.inv_ref
  168.8 34.4 %backward.1 = (bf16[256,2560]{1,0:T(8,128)(2,1)}, bf16[512,2560]{1,0:T(8,128)(2,1)}, bf16[512,2560]{1,0:T(8,128)(2,1)}, bf16[512,2560]{1,0:T(8,128)(2,1)}, bf16[...) custom-call(s32[12]{0:T(128)} %reshape.13.where_ref, ...), custom_call_target="tpu_custom_call" | custom-call | flops 4026531840 | bytes 62914560 | tf_op jit(solution)/shard_map/backward/pallas_call | solution.py:199
  203.2 130.6 %scatter.1 = bf16[512,2560]{1,0:T(8,128)(2,1)} custom-call(bf16[512,2560]{1,0:T(8,128)(2,1)} %get-tuple-element.36.refs_0_, bf16[512,2560]{1,0:T(8,128)(2,1)} %get-tuple-element.37.refs_1_, bf16[512,2560]{1,0:T(8,128)(2,1)} %get-tuple-element.38.refs_2_, bf16[512,2560]{1,0:T(8,128)(2,1)} %get-tuple-element.39.refs_3_, ...), custom_call_target="tpu_custom_call" | custom-call | tf_op jit(solution)/shard_map/scatter/pallas_call | solution.py:550
  333.8 3.4 fusion.9
  (1 shorter events, 0.0 us)
Async XLA Ops:
  2.7 2.9 copy-start.1
  5.7 1.5 copy-start
